TPU v7x, 32 devices: a whole 2x2x4 slice. The times are simulated.
32 devices in a mesh: gx: 8 (over z, x), gy: 4 (over y, core).
Axes of the slice: x: 2, y: 2, z: 4, core: 2. Of those that a mesh axis runs over, the one named last changes fastest.
Arguments:
- electric: float32 [3, 256, 64, 128], P(None, 'gx', 'gy'), may hold values from -6 to 6
- magnetic: float32 [3, 256, 64, 128], P(None, 'gx', 'gy'), may hold values from -6 to 6
- material: int32 [256, 64, 128], P('gx', 'gy'), may hold values from 0 to 3
- pml_flags: int32 [256, 64, 128], P('gx', 'gy'), may hold values 0 or 1
- permittivity: float32 [4], replicated, may hold values from 1 to 12
- pml_sigma: float32 [128], replicated, may hold values from 0.05 to 1
- omega: float32 [8], replicated, may hold values from 0.5 to 3
Outputs:
- electric_out: float32 [3, 256, 64, 128], P(None, 'gx', 'gy')
- magnetic_out: float32 [3, 256, 64, 128], P(None, 'gx', 'gy')
- spectra: float32 [16, 2, 256, 64], P('gy', None, 'gx')
All inputs are finite; a program needn't handle non-finite values. No bound on the sum of `pml_flags` on one device may be relied on, other than what follows from the above.
Results may differ from a plain program's by a relative error of at most 0.00002.
Values sent between devices are 32-bit elements; how exact they have to be, the bound alone decides.
A program may use at most 64 MiB of HBM per device.

v0:
```python
import jax
import jax.numpy as jnp
from jax import lax
from jax.sharding import PartitionSpec as P

STEPS = 2
NFREQ = 8
NMAT = 4


time_step = 0.5


def from_behind(x, axis, by):
    devices = lax.axis_size(axis)
    pairs = [(i, i + by) for i in range(devices) if 0 <= i + by < devices]
    return lax.ppermute(x, axis, pairs)


def forward_diff(field, rim, axis):
    rest = lax.slice_in_dim(field, 1, field.shape[axis], axis=axis)
    return jnp.concatenate([rest, rim], axis=axis) - field


def backward_diff(field, rim, axis):
    rest = lax.slice_in_dim(field, 0, field.shape[axis] - 1, axis=axis)
    return field - jnp.concatenate([rim, rest], axis=axis)


def zero_rim(field, axis):
    return jnp.zeros_like(lax.slice_in_dim(field, 0, 1, axis=axis))


def coefficients(eps_cell, sigma_cell):
    s_mag = sigma_cell * time_step / 2.0
    h_keep = (1.0 - s_mag) / (1.0 + s_mag)
    h_gain = time_step / (1.0 + s_mag)
    s_ele = sigma_cell * time_step / (2.0 * eps_cell)
    e_keep = (1.0 - s_ele) / (1.0 + s_ele)
    e_gain = time_step / (eps_cell * (1.0 + s_ele))
    return (h_keep, h_gain, e_keep, e_gain)


def local(electric, magnetic, material, pml_flags, permittivity, pml_sigma, omega):
    eps_cell = jnp.zeros(material.shape, jnp.float32)
    for index in range(NMAT):
        eps_cell = eps_cell + (material == index).astype(jnp.float32) * permittivity[index]
    sigma_cell = pml_flags.astype(jnp.float32) * pml_sigma[None, None, :]
    plane_at = electric.shape[3] // 2
    slots_total = 2 * NFREQ
    coef_rows = []
    samples = []
    for step in range(STEPS):
        moment = (step + 1) * time_step
        coef_rows.append(jnp.concatenate([jnp.cos(omega * moment), -jnp.sin(omega * moment)]))
    h_keep, h_gain, e_keep, e_gain = coefficients(eps_cell, sigma_cell)
    for step in range(STEPS):
        ex, ey, ez = (electric[0], electric[1], electric[2])
        zero_z = zero_rim(ex, 2)
        rim_x = from_behind(jnp.stack([ey[:1], ez[:1]]), "gx", -1)
        rim_y = from_behind(jnp.stack([ex[:, :1], ez[:, :1]]), "gy", -1)
        curl_x = forward_diff(ez, rim_y[1], 1) - forward_diff(ey, zero_z, 2)
        curl_y = forward_diff(ex, zero_z, 2) - forward_diff(ez, rim_x[1], 0)
        curl_z = forward_diff(ey, rim_x[0], 0) - forward_diff(ex, rim_y[0], 1)
        magnetic = h_keep[None] * magnetic - h_gain[None] * jnp.stack([curl_x, curl_y, curl_z])
        hx, hy, hz = (magnetic[0], magnetic[1], magnetic[2])
        last_x = hx.shape[0] - 1
        last_y = hx.shape[1] - 1
        rim_hx = from_behind(jnp.stack([hy[last_x:], hz[last_x:]]), "gx", 1)
        rim_hy = from_behind(jnp.stack([hx[:, last_y:], hz[:, last_y:]]), "gy", 1)
        curl_x = backward_diff(hz, rim_hy[1], 1) - backward_diff(hy, zero_z, 2)
        curl_y = backward_diff(hx, zero_z, 2) - backward_diff(hz, rim_hx[1], 0)
        curl_z = backward_diff(hy, rim_hx[0], 0) - backward_diff(hx, rim_hy[0], 1)
        electric = e_keep[None] * electric + e_gain[None] * jnp.stack([curl_x, curl_y, curl_z])
        samples.append(electric[0:2, :, :, plane_at])
    coef_table = jnp.stack(coef_rows)
    partial_sums = jnp.zeros((slots_total,) + samples[0].shape, jnp.float32)
    for step in range(STEPS):
        partial_sums = partial_sums + coef_table[step][:, None, None, None] * samples[step][None]
    spectra = lax.all_to_all(partial_sums, "gy", split_axis=0, concat_axis=3, tiled=True)
    return (electric, magnetic, spectra)


def solution(mesh):
    placed = (
        P(None, "gx", "gy", None),
        P(None, "gx", "gy", None),
        P("gx", "gy", None),
        P("gx", "gy", None),
        P(),
        P(),
        P(),
    )
    return jax.shard_map(
        local,
        mesh=mesh,
        in_specs=placed,
        out_specs=(P(None, "gx", "gy", None), P(None, "gx", "gy", None), P("gy", None, "gx", None)),
        check_vma=False,
    )
```

profile of v0, /device:TPU:0, one launch (start us, length us, event | category | flops | bytes accessed | tf_op | source)
XLA Modules:
  0.0 60.3 jit_solution(365923145963021683)
XLA Ops:
  0.6 1.2 %fusion.27 = (f32[1,32,16,128]{3,2,1,0:T(8,128)S(1)}, f32[1,32,16,128]{3,2,1,0:T(8,128)S(1)}, f32[32,16,128]{2,1,0:T(8,128)S(1)}) fusion(f32[3,32,16,128]{3,2,1,0:T(8,128)} %param.7), kind=kLoop, calls=%fused_computation.91 | loop fusion | bytes 1572864 | tf_op jit(solution)/shard_map/slice | solution.py:58
  2.1 1.3 %collective-permute-start = (f32[2,32,1,128]{3,2,1,0:T(1,128)S(1)}, f32[2,32,1,128]{3,2,1,0:T(1,128)S(1)}, u32[]{:S(2)}, u32[]{:S(2)}) collective-permute-start(f32[2,32,1,128]{3,2,1,0:T(1,128)S(1)} %pad_maximum_fusion), channel_id=1, source_target_pairs={{1,0},{2,1},{3,2},{5,4},{6,5},{7,6},{9,8},{10,9},{11,10},{13,12},{... | collective-permute-start | bytes 98312 | tf_op jit(solution)/shard_map/ppermute | solution.py:17
  3.4 1.3 %collective-permute-start.1 = (f32[2,1,16,128]{3,2,1,0:T(8,128)S(1)}, f32[2,1,16,128]{3,2,1,0:T(8,128)S(1)}, u32[]{:S(2)}, u32[]{:S(2)}) collective-permute-start(f32[2,1,16,128]{3,2,1,0:T(8,128)S(1)} %stack.100), channel_id=1, source_target_pairs={{4,0},{8,4},{12,8},{16,12},{20,16},{24,20},{28,24},{5,1},{9,5},{13... | collective-permute-start | bytes 49160 | tf_op jit(solution)/shard_map/ppermute | solution.py:17
  4.8 0.5 copy-done.24
  5.3 0.6 fusion.33
  6.1 0.6 %copy-done.25 = f32[128]{0:T(128)S(1)} copy-done((f32[128]{0:T(128)S(1)}, f32[128]{0:T(128)}, u32[]{:S(2)}) %copy-start.25) | copy-done | bytes 536
  6.7 2.8 %subtract_divide_fusion.1 = (f32[32,16,128]{2,1,0:T(8,128)S(1)}, f32[32,16,128]{2,1,0:T(8,128)S(1)}, f32[32,16,128]{2,1,0:T(8,128)S(1)}, f32[32,16,128]{2,1,0:T(8,128)S(1)}) fusion(f32[]{:T(128)} %bitcast.3, s32[32,16,128]{2,1,0:T(8,128)S(1)} %copy-done.22, f32[]{:T(128)} %bitcast.2, f32[]{:T(128)} %bitcast.1, f32[]{:T(128)} %bitcast, f32[128]{0:T(128)S(1)} %copy-done.25, ...), kind=kLoop, calls=%fused_computation.56 | loop fusion | flops 1703936 | bytes 1573392 | tf_op jit(solution)/shard_map/div | solution.py:39
  10.3 0.3 fusion.5
  11.0 0.2 fusion.8
  11.2 0.3 copy-done.3
  11.5 0.2 copy-done.5
  11.7 0.6 copy-done.2
  12.6 5.5 %collective-permute-start.3 = (f32[2,1,16,128]{3,2,1,0:T(8,128)S(1)}, f32[2,1,16,128]{3,2,1,0:T(8,128)S(1)}, u32[]{:S(2)}, u32[]{:S(2)}) collective-permute-start(f32[2,1,16,128]{3,2,1,0:T(8,128)S(1)} %stack.124), channel_id=1, source_target_pairs={{0,4},{4,8},{8,12},{12,16},{16,20},{20,24},{24,28},{1,5},{5,9},{9,... | collective-permute-start | bytes 49160 | tf_op jit(solution)/shard_map/ppermute | solution.py:17
  18.1 2.8 %collective-permute-start.2 = (f32[2,32,1,128]{3,1,2,0:T(8,128)S(1)}, f32[2,32,1,128]{3,1,2,0:T(8,128)S(1)}, u32[]{:S(2)}, u32[]{:S(2)}) collective-permute-start(f32[2,32,1,128]{3,1,2,0:T(8,128)S(1)} %pad_maximum_fusion.1), channel_id=1, source_target_pairs={{0,1},{1,2},{2,3},{4,5},{5,6},{6,7},{8,9},{9,10},{10,11},{12,13},{... | collective-permute-start | bytes 98312 | tf_op jit(solution)/shard_map/ppermute | solution.py:17
  20.9 0.8 %collective-permute-done.2 = f32[2,32,1,128]{3,1,2,0:T(8,128)S(1)} collective-permute-done((f32[2,32,1,128]{3,1,2,0:T(8,128)S(1)}, f32[2,32,1,128]{3,1,2,0:T(8,128)S(1)}, u32[]{:S(2)}, u32[]{:S(2)}) %collective-permute-start.2) | collective-permute-done | bytes 32800 | tf_op jit(solution)/shard_map/ppermute | solution.py:17
  21.8 0.3 fusion.10
  22.5 0.7 %slice_bitcast_fusion.14 = f32[1,32,15,128]{3,1,2,0:T(8,128)} fusion(f32[32,16,128]{2,0,1:T(8,128)S(1)} %bitcast.147), kind=kLoop, calls=%fused_computation.74 | loop fusion | bytes 491520 | tf_op jit(solution)/shard_map/concatenate | solution.py:22
  23.2 0.8 %slice_bitcast_fusion.6 = (f32[31,16,128]{2,1,0:T(8,128)}, f32[1,31,16,128]{3,2,1,0:T(8,128)}) fusion(f32[3,32,16,128]{3,2,1,0:T(8,128)S(1)} %fusion.1), kind=kLoop, calls=%fused_computation.61 | loop fusion | bytes 1015808 | tf_op jit(solution)/shard_map/slice | solution.py:21
  24.0 0.8 %pad_subtract_fusion.1 = f32[32,16,128]{2,0,1:T(8,128)} fusion(f32[32,16,127]{2,0,1:T(8,128)S(1)} %slice.353, f32[1,32,16,128]{3,2,1,0:T(8,128)S(1)} %get-tuple-element.23), kind=kLoop, calls=%fused_computation.53 | loop fusion | flops 65536 | bytes 784384 | tf_op jit(solution)/shard_map/sub | solution.py:22
  24.9 1.3 %collective-permute-start.5 = (f32[2,1,16,128]{3,2,1,0:T(8,128)S(1)}, f32[2,1,16,128]{3,2,1,0:T(8,128)S(1)}, u32[]{:S(2)}, u32[]{:S(2)}) collective-permute-start(f32[2,1,16,128]{3,2,1,0:T(8,128)S(1)} %stack.125), channel_id=1, source_target_pairs={{4,0},{8,4},{12,8},{16,12},{20,16},{24,20},{28,24},{5,1},{9,5},{13... | collective-permute-start | bytes 49160 | tf_op jit(solution)/shard_map/ppermute | solution.py:17
  26.2 0.7 %slice.346 = f32[32,15,128]{2,1,0:T(8,128)} slice(f32[32,16,128]{2,1,0:T(8,128)S(1)} %get-tuple-element.24), slice={[0:32], [1:16], [0:128]} | slice | bytes 491520 | tf_op jit(solution)/shard_map/slice | solution.py:21
  26.9 1.0 %slice.375 = f32[2,32,16,1]{3,2,1,0:T(8,128)} slice(f32[3,32,16,128]{3,2,1,0:T(8,128)S(1)} %fusion.1), slice={[0:2], [0:32], [0:16], [64:65]} | slice | bytes 8192 | tf_op jit(solution)/shard_map/slice | solution.py:75
  27.9 1.3 %collective-permute-start.4 = (f32[2,32,1,128]{3,1,2,0:T(8,128)S(1)}, f32[2,32,1,128]{3,1,2,0:T(8,128)S(1)}, u32[]{:S(2)}, u32[]{:S(2)}) collective-permute-start(f32[2,32,1,128]{3,1,2,0:T(8,128)S(1)} %pad_maximum_fusion.2), channel_id=1, source_target_pairs={{1,0},{2,1},{3,2},{5,4},{6,5},{7,6},{9,8},{10,9},{11,10},{13,12},{... | collective-permute-start | bytes 98312 | tf_op jit(solution)/shard_map/ppermute | solution.py:17
  29.2 1.3 %copy.94 = f32[2,32,16,1]{1,2,3,0:T(8,128)S(1)} copy(f32[2,32,16,1]{3,2,1,0:T(8,128)} %slice.375) | data formatting | bytes 8192 | tf_op jit(solution)/shard_map/slice | solution.py:75
  30.5 0.6 %collective-permute-done.5 = f32[2,1,16,128]{3,2,1,0:T(8,128)S(1)} collective-permute-done((f32[2,1,16,128]{3,2,1,0:T(8,128)S(1)}, f32[2,1,16,128]{3,2,1,0:T(8,128)S(1)}, u32[]{:S(2)}, u32[]{:S(2)}) %collective-permute-start.5) | collective-permute-done | bytes 16416 | tf_op jit(solution)/shard_map/ppermute | solution.py:17
  31.1 1.5 %collective-permute-done.4 = f32[2,32,1,128]{3,1,2,0:T(8,128)S(1)} collective-permute-done((f32[2,32,1,128]{3,1,2,0:T(8,128)S(1)}, f32[2,32,1,128]{3,1,2,0:T(8,128)S(1)}, u32[]{:S(2)}, u32[]{:S(2)}) %collective-permute-start.4) | collective-permute-done | bytes 32800 | tf_op jit(solution)/shard_map/ppermute | solution.py:17
  32.6 1.1 %maximum_subtract_fusion.11 = f32[1,32,16,128]{3,1,2,0:T(8,128)S(1)} fusion(f32[1,32,1,128]{3,1,2,0:T(8,128)S(1)} %get-tuple-element.49, f32[1,32,15,128]{3,1,2,0:T(8,128)} %slice_bitcast_fusion.14, f32[1,32,16,128]{3,2,1,0:T(8,128)S(1)} %get-tuple-element.23), kind=kLoop, calls=%fused_computation.39 | loop fusion | flops 131072 | bytes 786432 | tf_op jit(solution)/shard_map/sub | solution.py:22
  33.7 0.2 slice_bitcast_fusion.9
  34.1 0.6 copy-done.21
  34.7 0.2 copy-done.18
  35.0 0.2 fusion.15
  35.2 0.7 %copy-done.4 = f32[1,32,16,128]{3,2,1,0:T(8,128)S(1)} copy-done((f32[1,32,16,128]{3,2,1,0:T(8,128)S(1)}, f32[1,32,16,128]{3,2,1,0:T(8,128)}, u32[]{:S(2)}) %copy-start.4) | copy-done | bytes 262168
  36.2 0.2 fusion.2
  36.8 4.9 %collective-permute-start.7 = (f32[2,1,16,128]{3,2,1,0:T(8,128)S(1)}, f32[2,1,16,128]{3,2,1,0:T(8,128)S(1)}, u32[]{:S(2)}, u32[]{:S(2)}) collective-permute-start(f32[2,1,16,128]{3,2,1,0:T(8,128)S(1)} %stack.126), channel_id=1, source_target_pairs={{0,4},{4,8},{8,12},{12,16},{16,20},{20,24},{24,28},{1,5},{5,9},{9,... | collective-permute-start | bytes 49160 | tf_op jit(solution)/shard_map/ppermute | solution.py:17
  41.8 4.8 %collective-permute-start.6 = (f32[2,32,1,128]{3,1,2,0:T(8,128)S(1)}, f32[2,32,1,128]{3,1,2,0:T(8,128)S(1)}, u32[]{:S(2)}, u32[]{:S(2)}) collective-permute-start(f32[2,32,1,128]{3,1,2,0:T(8,128)S(1)} %pad_maximum_fusion.3), channel_id=1, source_target_pairs={{0,1},{1,2},{2,3},{4,5},{5,6},{6,7},{8,9},{9,10},{10,11},{12,13},{... | collective-permute-start | bytes 98312 | tf_op jit(solution)/shard_map/ppermute | solution.py:17
  46.6 0.8 %collective-permute-done.6 = f32[2,32,1,128]{3,1,2,0:T(8,128)S(1)} collective-permute-done((f32[2,32,1,128]{3,1,2,0:T(8,128)S(1)}, f32[2,32,1,128]{3,1,2,0:T(8,128)S(1)}, u32[]{:S(2)}, u32[]{:S(2)}) %collective-permute-start.6) | collective-permute-done | bytes 32800 | tf_op jit(solution)/shard_map/ppermute | solution.py:17
  47.6 0.2 slice_bitcast_fusion.8
  47.8 0.2 fusion.20
  48.1 0.7 %copy-done.8 = f32[32,16,128]{2,1,0:T(8,128)S(1)} copy-done((f32[32,16,128]{2,1,0:T(8,128)S(1)}, f32[32,16,128]{2,1,0:T(8,128)}, u32[]{:S(2)}) %copy-start.8) | copy-done | bytes 262168
  48.8 0.2 fusion.3
  49.0 0.2 slice.376
  49.2 0.3 copy.95
  49.5 0.4 copy-done.17
  50.0 0.2 reshape.67
  50.2 7.8 %all_to_all.18 = f32[4,1,4096]{2,1,0:T(1,128)S(1)} all-to-all(f32[4,1,4096]{2,1,0:T(1,128)S(1)} %reshape.67), channel_id=1, replica_groups=mesh['gx'=8,'gy'=4] {'gy'}, dimensions={0} | all-to-all | bytes 131072 | tf_op jit(solution)/shard_map/all_to_all | solution.py:80
  58.0 0.5 broadcast.76
  58.5 0.8 %reduce = f32[4,4096]{1,0:T(4,128)S(1)} reduce(f32[4,1,4096]{2,1,0:T(1,128)S(1)} %all_to_all.18, f32[]{:T(128)} %broadcast.76), dimensions={1}, to_apply=%all_to_all.13.reduce_sub_computation | reduce | bytes 131076 | tf_op jit(solution)/shard_map/all_to_all | solution.py:80
  59.5 0.8 %copy.97 = f32[4,2,32,64]{3,2,1,0:T(8,128)} copy(f32[4,2,32,64]{2,3,1,0:T(8,128)S(1)} %bitcast.156) | data formatting | bytes 131072
  (106 shorter events, 3.6 us)
Async XLA Ops:
  0.6 2.7 %copy-start = (f32[3,32,16,128]{3,2,1,0:T(8,128)S(1)}, f32[3,32,16,128]{3,2,1,0:T(8,128)}, u32[]{:S(2)}) copy-start(f32[3,32,16,128]{3,2,1,0:T(8,128)} %param.7) | copy-start | bytes 2359300
  2.1 8.3 %collective-permute-start = (f32[2,32,1,128]{3,2,1,0:T(1,128)S(1)}, f32[2,32,1,128]{3,2,1,0:T(1,128)S(1)}, u32[]{:S(2)}, u32[]{:S(2)}) collective-permute-start(f32[2,32,1,128]{3,2,1,0:T(1,128)S(1)} %pad_maximum_fusion), channel_id=1, source_target_pairs={{1,0},{2,1},{3,2},{5,4},{6,5},{7,6},{9,8},{10,9},{11,10},{13,12},{... | collective-permute-start | bytes 98312 | tf_op jit(solution)/shard_map/ppermute | solution.py:17
  3.4 6.7 %collective-permute-start.1 = (f32[2,1,16,128]{3,2,1,0:T(8,128)S(1)}, f32[2,1,16,128]{3,2,1,0:T(8,128)S(1)}, u32[]{:S(2)}, u32[]{:S(2)}) collective-permute-start(f32[2,1,16,128]{3,2,1,0:T(8,128)S(1)} %stack.100), channel_id=1, source_target_pairs={{4,0},{8,4},{12,8},{16,12},{20,16},{24,20},{28,24},{5,1},{9,5},{13... | collective-permute-start | bytes 49160 | tf_op jit(solution)/shard_map/ppermute | solution.py:17
  4.7 0.7 %copy-start.24 = (f32[4]{0:T(128)S(1)}, f32[4]{0:T(128)}, u32[]{:S(2)}) copy-start(f32[4]{0:T(128)} %param.11) | copy-start | bytes 52
  4.7 1.3 %copy-start.22 = (s32[32,16,128]{2,1,0:T(8,128)S(1)}, s32[32,16,128]{2,1,0:T(8,128)}, u32[]{:S(2)}) copy-start(s32[32,16,128]{2,1,0:T(8,128)} %param.9) | copy-start | bytes 786436
  4.7 1.3 %copy-start.23 = (s32[32,16,128]{2,1,0:T(8,128)S(1)}, s32[32,16,128]{2,1,0:T(8,128)}, u32[]{:S(2)}) copy-start(s32[32,16,128]{2,1,0:T(8,128)} %param.10) | copy-start | bytes 786436
  5.3 0.7 %copy-start.26 = (f32[8]{0:T(128)S(1)}, f32[8]{0:T(128)}, u32[]{:S(2)}) copy-start(f32[8]{0:T(128)} %param.13) | copy-start | bytes 100
  6.0 0.7 %copy-start.25 = (f32[128]{0:T(128)S(1)}, f32[128]{0:T(128)}, u32[]{:S(2)}) copy-start(f32[128]{0:T(128)} %param.12) | copy-start | bytes 1540
  9.5 1.8 %copy-start.11 = (f32[32,16,128]{2,1,0:T(8,128)}, f32[32,16,128]{2,1,0:T(8,128)S(1)}, u32[]{:S(2)}) copy-start(f32[32,16,128]{2,1,0:T(8,128)S(1)} %get-tuple-element.40) | copy-start | bytes 786436
  9.5 1.8 %copy-start.13 = (f32[32,16,128]{2,1,0:T(8,128)}, f32[32,16,128]{2,1,0:T(8,128)S(1)}, u32[]{:S(2)}) copy-start(f32[32,16,128]{2,1,0:T(8,128)S(1)} %get-tuple-element.41) | copy-start | bytes 786436
  9.5 12.5 %copy-start.7 = (f32[32,16,128]{2,1,0:T(8,128)}, f32[32,16,128]{2,1,0:T(8,128)S(1)}, u32[]{:S(2)}) copy-start(f32[32,16,128]{2,1,0:T(8,128)S(1)} %get-tuple-element.38) | copy-start | bytes 786436
  9.5 12.5 %copy-start.9 = (f32[32,16,128]{2,1,0:T(8,128)}, f32[32,16,128]{2,1,0:T(8,128)S(1)}, u32[]{:S(2)}) copy-start(f32[32,16,128]{2,1,0:T(8,128)S(1)} %get-tuple-element.39) | copy-start | bytes 786436
  10.8 0.7 %copy-start.3 = (f32[1,32,16,128]{3,2,1,0:T(8,128)}, f32[1,32,16,128]{3,2,1,0:T(8,128)S(1)}, u32[]{:S(2)}) copy-start(f32[1,32,16,128]{3,2,1,0:T(8,128)S(1)} %copy.81) | copy-start | bytes 786436
  10.8 1.4 %copy-start.2 = (f32[3,32,16,128]{3,2,1,0:T(8,128)S(1)}, f32[3,32,16,128]{3,2,1,0:T(8,128)}, u32[]{:S(2)}) copy-start(f32[3,32,16,128]{3,2,1,0:T(8,128)} %param.8) | copy-start | bytes 2359300
  11.0 0.7 %copy-start.5 = (f32[1,32,16,128]{3,2,1,0:T(8,128)}, f32[1,32,16,128]{3,2,1,0:T(8,128)S(1)}, u32[]{:S(2)}) copy-start(f32[1,32,16,128]{3,2,1,0:T(8,128)S(1)} %copy.82) | copy-start | bytes 786436
  11.2 1.2 %copy-start.15 = (f32[1,32,16,128]{3,2,1,0:T(8,128)}, f32[1,32,16,128]{3,2,1,0:T(8,128)S(1)}, u32[]{:S(2)}) copy-start(f32[1,32,16,128]{3,2,1,0:T(8,128)S(1)} %fusion.8) | copy-start | bytes 786436
  12.6 8.3 %collective-permute-start.3 = (f32[2,1,16,128]{3,2,1,0:T(8,128)S(1)}, f32[2,1,16,128]{3,2,1,0:T(8,128)S(1)}, u32[]{:S(2)}, u32[]{:S(2)}) collective-permute-start(f32[2,1,16,128]{3,2,1,0:T(8,128)S(1)} %stack.124), channel_id=1, source_target_pairs={{0,4},{4,8},{8,12},{12,16},{16,20},{20,24},{24,28},{1,5},{5,9},{9,... | collective-permute-start | bytes 49160 | tf_op jit(solution)/shard_map/ppermute | solution.py:17
  18.1 3.6 %collective-permute-start.2 = (f32[2,32,1,128]{3,1,2,0:T(8,128)S(1)}, f32[2,32,1,128]{3,1,2,0:T(8,128)S(1)}, u32[]{:S(2)}, u32[]{:S(2)}) collective-permute-start(f32[2,32,1,128]{3,1,2,0:T(8,128)S(1)} %pad_maximum_fusion.1), channel_id=1, source_target_pairs={{0,1},{1,2},{2,3},{4,5},{5,6},{6,7},{8,9},{9,10},{10,11},{12,13},{... | collective-permute-start | bytes 98312 | tf_op jit(solution)/shard_map/ppermute | solution.py:17
  24.9 6.3 %collective-permute-start.5 = (f32[2,1,16,128]{3,2,1,0:T(8,128)S(1)}, f32[2,1,16,128]{3,2,1,0:T(8,128)S(1)}, u32[]{:S(2)}, u32[]{:S(2)}) collective-permute-start(f32[2,1,16,128]{3,2,1,0:T(8,128)S(1)} %stack.125), channel_id=1, source_target_pairs={{4,0},{8,4},{12,8},{16,12},{20,16},{24,20},{28,24},{5,1},{9,5},{13... | collective-permute-start | bytes 49160 | tf_op jit(solution)/shard_map/ppermute | solution.py:17
  27.9 4.7 %collective-permute-start.4 = (f32[2,32,1,128]{3,1,2,0:T(8,128)S(1)}, f32[2,32,1,128]{3,1,2,0:T(8,128)S(1)}, u32[]{:S(2)}, u32[]{:S(2)}) collective-permute-start(f32[2,32,1,128]{3,1,2,0:T(8,128)S(1)} %pad_maximum_fusion.2), channel_id=1, source_target_pairs={{1,0},{2,1},{3,2},{5,4},{6,5},{7,6},{9,8},{10,9},{11,10},{13,12},{... | collective-permute-start | bytes 98312 | tf_op jit(solution)/shard_map/ppermute | solution.py:17
  32.6 1.1 %copy-start.20 = (f32[1,31,16,128]{3,2,1,0:T(8,128)S(1)}, f32[1,31,16,128]{3,2,1,0:T(8,128)}, u32[]{:S(2)}) copy-start(f32[1,31,16,128]{3,2,1,0:T(8,128)} %get-tuple-element.22) | copy-start | bytes 761860
  33.7 0.9 %copy-start.21 = (f32[31,16,128]{2,1,0:T(8,128)S(1)}, f32[31,16,128]{2,1,0:T(8,128)}, u32[]{:S(2)}) copy-start(f32[31,16,128]{2,1,0:T(8,128)} %get-tuple-element.21) | copy-start | bytes 761860
  33.9 1.0 %copy-start.18 = (f32[32,16,128]{2,0,1:T(8,128)S(1)}, f32[32,16,128]{2,0,1:T(8,128)}, u32[]{:S(2)}) copy-start(f32[32,16,128]{2,0,1:T(8,128)} %pad_subtract_fusion.1) | copy-start | bytes 786436
  33.9 1.0 %copy-start.19 = (f32[32,15,128]{2,1,0:T(8,128)S(1)}, f32[32,15,128]{2,1,0:T(8,128)}, u32[]{:S(2)}) copy-start(f32[32,15,128]{2,1,0:T(8,128)} %slice.346) | copy-start | bytes 737284
  35.0 0.9 %copy-start.4 = (f32[1,32,16,128]{3,2,1,0:T(8,128)S(1)}, f32[1,32,16,128]{3,2,1,0:T(8,128)}, u32[]{:S(2)}) copy-start(f32[1,32,16,128]{3,2,1,0:T(8,128)} %copy-done.3) | copy-start | bytes 786436
  35.0 1.0 %copy-start.6 = (f32[1,32,16,128]{3,2,1,0:T(8,128)S(1)}, f32[1,32,16,128]{3,2,1,0:T(8,128)}, u32[]{:S(2)}) copy-start(f32[1,32,16,128]{3,2,1,0:T(8,128)} %copy-done.5) | copy-start | bytes 786436
  35.0 1.1 %copy-start.12 = (f32[32,16,128]{2,1,0:T(8,128)S(1)}, f32[32,16,128]{2,1,0:T(8,128)}, u32[]{:S(2)}) copy-start(f32[32,16,128]{2,1,0:T(8,128)} %copy-done.11) | copy-start | bytes 786436
  35.0 1.2 %copy-start.14 = (f32[32,16,128]{2,1,0:T(8,128)S(1)}, f32[32,16,128]{2,1,0:T(8,128)}, u32[]{:S(2)}) copy-start(f32[32,16,128]{2,1,0:T(8,128)} %copy-done.13) | copy-start | bytes 786436
  35.0 1.3 %copy-start.16 = (f32[1,32,16,128]{3,2,1,0:T(8,128)S(1)}, f32[1,32,16,128]{3,2,1,0:T(8,128)}, u32[]{:S(2)}) copy-start(f32[1,32,16,128]{3,2,1,0:T(8,128)} %copy-done.15) | copy-start | bytes 786436
  36.4 11.4 %copy-start.1 = (f32[3,32,16,128]{3,2,1,0:T(8,128)}, f32[3,32,16,128]{3,2,1,0:T(8,128)S(1)}, u32[]{:S(2)}) copy-start(f32[3,32,16,128]{3,2,1,0:T(8,128)S(1)} %fusion.2) | copy-start | bytes 2359300
  36.8 9.8 %collective-permute-start.7 = (f32[2,1,16,128]{3,2,1,0:T(8,128)S(1)}, f32[2,1,16,128]{3,2,1,0:T(8,128)S(1)}, u32[]{:S(2)}, u32[]{:S(2)}) collective-permute-start(f32[2,1,16,128]{3,2,1,0:T(8,128)S(1)} %stack.126), channel_id=1, source_target_pairs={{0,4},{4,8},{8,12},{12,16},{16,20},{20,24},{24,28},{1,5},{5,9},{9,... | collective-permute-start | bytes 49160 | tf_op jit(solution)/shard_map/ppermute | solution.py:17
  41.8 5.7 %collective-permute-start.6 = (f32[2,32,1,128]{3,1,2,0:T(8,128)S(1)}, f32[2,32,1,128]{3,1,2,0:T(8,128)S(1)}, u32[]{:S(2)}, u32[]{:S(2)}) collective-permute-start(f32[2,32,1,128]{3,1,2,0:T(8,128)S(1)} %pad_maximum_fusion.3), channel_id=1, source_target_pairs={{0,1},{1,2},{2,3},{4,5},{5,6},{6,7},{8,9},{9,10},{10,11},{12,13},{... | collective-permute-start | bytes 98312 | tf_op jit(solution)/shard_map/ppermute | solution.py:17
  47.8 1.0 %copy-start.8 = (f32[32,16,128]{2,1,0:T(8,128)S(1)}, f32[32,16,128]{2,1,0:T(8,128)}, u32[]{:S(2)}) copy-start(f32[32,16,128]{2,1,0:T(8,128)} %copy-done.7) | copy-start | bytes 786436
  47.8 1.0 %copy-start.10 = (f32[32,16,128]{2,1,0:T(8,128)S(1)}, f32[32,16,128]{2,1,0:T(8,128)}, u32[]{:S(2)}) copy-start(f32[32,16,128]{2,1,0:T(8,128)} %copy-done.9) | copy-start | bytes 786436
  49.0 0.9 %copy-start.17 = (f32[3,32,16,128]{3,2,1,0:T(8,128)}, f32[3,32,16,128]{3,2,1,0:T(8,128)S(1)}, u32[]{:S(2)}) copy-start(f32[3,32,16,128]{3,2,1,0:T(8,128)S(1)} %fusion.3) | copy-start | bytes 2359300
where the time goes:
time: 60.9 us; the launch traced here: 60.3 us
  starting transfers between devices  23.1 us (38%)
  local copies, waits for them, and re-layouts  15.7 us (26%)
  other arithmetic  8.49 us (14%)
  blocking collectives  7.84 us (13%)
  waiting for transfers between devices  3.74 us (6%)
  between operations  1.41 us (2%)
    ppermute x8, starting transfers between devices, from_behind(): return lax.ppermute(x, axis, pairs)  23.1 us
    all_to_all x1, blocking collectives, local(): lax.all_to_all(partial_sums, 'gy', split_axis=0, concat_axis=3, tiled=True)  7.84 us
    unnamed x64, local copies, waits for them, and re-layouts  7 us
    ppermute x8, waiting for transfers between devices, from_behind(): return lax.ppermute(x, axis, pairs)  3.74 us
    slice x4, local copies, waits for them, and re-layouts, local(): samples.append(electric[0:2, :, :, plane_at])  2.8 us
    div x1, other arithmetic, coefficients(): e_keep = (1.0 - s_ele) / (1.0 + s_ele)  2.75 us
    slice x8, local copies, waits for them, and re-layouts, forward_diff(): rest = lax.slice_in_dim(field, 1, field.shape[axis], axis=axis)  2.1 us
    sub x2, other arithmetic, forward_diff(): return jnp.concatenate([rest, rim], axis=axis) - field  1.92 us
  transfers between devices with their start and end apart: 8, of which 4 were waited for; matrix products, arithmetic and copies ran while one was open for 12% of the time, Pallas kernels for 0%

commit v1 on v0

v1 whole, which is shorter than its diff:
```python
import functools

import jax
import jax.numpy as jnp
from jax import lax
from jax.experimental import pallas as pl
from jax.experimental.pallas import tpu as pltpu
from jax.sharding import PartitionSpec as P

STEPS = 2
NFREQ = 8
NMAT = 4
DT = 0.5
MESH = pl.DeviceIdType.MESH

TOP = 8


def loop(low, high, unroll, body, carry):
    rounds = (high - low) // unroll

    def several(i, carry):
        for k in range(unroll):
            carry = body(low + i * unroll + k, carry)
        return carry

    carry = lax.fori_loop(0, rounds, several, carry)
    for p in range(low + rounds * unroll, high):
        carry = body(p, carry)
    return carry


def kernel(ngx, ngy, nx, ny, nz,
           e_in, h_in, mat_in, flag_in, perm_in, sigma_in, omega_in,
           e_out, h_out, spectra,
           e0, e1, hf, flag, mat, ek, eg, perm, sigma, omega, samp,
           load_sem, store_sem, send1, recv1, send2, recv2, send3, recv3):
    gx, gy = lax.axis_index("gx"), lax.axis_index("gy")
    left, right = gx > 0, gx < ngx - 1
    down, up = gy > 0, gy < ngy - 1
    own_x = pl.ds(1, nx)
    own_y = pl.ds(TOP, ny)
    behind, ahead = TOP - 1, TOP + ny
    last = nx + 1

    loads = [
        pltpu.make_async_copy(e_in, e0.at[:, own_x, own_y], load_sem.at[0]),
        pltpu.make_async_copy(h_in, hf.at[:, own_x, own_y], load_sem.at[1]),
        pltpu.make_async_copy(flag_in, flag.at[own_x, own_y], load_sem.at[2]),
        pltpu.make_async_copy(mat_in, mat, load_sem.at[3]),
        pltpu.make_async_copy(sigma_in, sigma, load_sem.at[4]),
    ]
    for copy in loads:
        copy.start()

    barrier = pltpu.get_barrier_semaphore()
    partners = [
        (left, (gx - 1, gy)),
        (right, (gx + 1, gy)),
        (left & up, (gx - 1, gy + 1)),
        (right & down, (gx + 1, gy - 1)),
    ]
    expected = ngy - 1
    for there, device in partners:
        expected = expected + there.astype(jnp.int32)

        @pl.when(there)
        def _():
            pl.semaphore_signal(barrier, inc=1, device_id=device, device_id_type=MESH)

    for d in range(1, ngy):
        pl.semaphore_signal(barrier, inc=1, device_id=(gx, lax.rem(gy + d, ngy)), device_id_type=MESH)

    @pl.when(jnp.logical_not(right))
    def _():
        for e in (e0, e1):
            for c in (1, 2):
                e[c, last, 0:ahead] = jnp.zeros((ahead, nz), jnp.float32)

    @pl.when(jnp.logical_not(up))
    def _():
        for e in (e0, e1):
            for c in (0, 2):
                e[c, 0:last, ahead:ahead + 8] = jnp.zeros((last, 8, nz), jnp.float32)

    pl.semaphore_wait(barrier, expected)

    def remote(src, dst, sends, recvs, i, device):
        return pltpu.make_async_remote_copy(
            src_ref=src, dst_ref=dst, send_sem=sends.at[i], recv_sem=recvs.at[i],
            device_id=device, device_id_type=MESH)

    def e_halo(src, x_of, y_of, e, sends, recvs):
        at = functools.partial(remote, sends=sends, recvs=recvs)
        xs = pl.ds(x_of(0), nx)
        ys = pl.ds(y_of(0), ny)
        to_left = [at(src.at[1:3, x_of(0), ys], e.at[1:3, last, own_y], i=0, device=(gx - 1, gy))]
        to_right = [at(src.at[:, x_of(nx - 1), ys], e.at[:, 0, own_y], i=1, device=(gx + 1, gy))]
        to_down = [at(src.at[c, xs, y_of(0)], e.at[c, own_x, ahead], i=2 + c // 2, device=(gx, gy - 1)) for c in (0, 2)]
        to_up = [at(src.at[:, xs, y_of(ny - 1)], e.at[:, own_x, behind], i=4, device=(gx, gy + 1))]
        corner_lu = [at(src.at[1, x_of(0), y_of(ny - 1)], e.at[1, last, behind], i=5, device=(gx - 1, gy + 1))]
        corner_rd = [at(src.at[0, x_of(nx - 1), y_of(0)], e.at[0, 0, ahead], i=6, device=(gx + 1, gy - 1))]
        return [
            [left, right, to_left],
            [right, left, to_right],
            [down, up, to_down],
            [up, down, to_up],
            [left & up, right & down, corner_lu],
            [right & down, left & up, corner_rd],
        ]

    def start(plan):
        for sends, _, copies in plan:
            @pl.when(sends)
            def _():
                for copy in copies:
                    copy.start()

    def wait_recv(plan):
        for _, receives, copies in plan:
            @pl.when(receives)
            def _():
                for copy in copies:
                    copy.wait_recv()

    def wait_send(plan):
        for sends, _, copies in plan:
            @pl.when(sends)
            def _():
                for copy in copies:
                    copy.wait_send()

    round1 = e_halo(e_in, lambda x: x, lambda y: y, e0, send1, recv1)
    at1 = functools.partial(remote, sends=send1, recvs=recv1)
    round1[1][2] += [
        at1(h_in.at[1:3, nx - 1], hf.at[1:3, 0, own_y], i=7, device=(gx + 1, gy)),
        at1(flag_in.at[nx - 1], flag.at[0, own_y], i=8, device=(gx + 1, gy)),
    ]
    round1[3][2] += [
        at1(h_in.at[0, :, ny - 1], hf.at[0, own_x, behind], i=9, device=(gx, gy + 1)),
        at1(h_in.at[2, :, ny - 1], hf.at[2, own_x, behind], i=10, device=(gx, gy + 1)),
        at1(flag_in.at[:, ny - 1], flag.at[own_x, behind], i=11, device=(gx, gy + 1)),
    ]
    start(round1)

    loads[4].wait()
    sg = sigma[...]
    sm = sg * DT / 2.0
    hk1 = (1.0 - sm) / (1.0 + sm)
    hg1 = DT / (1.0 + sm)
    ek1, eg1, eg0 = [], [], []
    for m in range(NMAT):
        eps = jnp.full((1, nz), perm_in[m], jnp.float32)
        se = sg * DT / (2.0 * eps)
        ek1.append((1.0 - se) / (1.0 + se))
        eg1.append(DT / (eps * (1.0 + se)))
        eg0.append(DT / eps)

    def lanes(n):
        return lax.broadcasted_iota(jnp.int32, (n, nz), 1)

    def next_z(f):
        return jnp.where(lanes(f.shape[0]) == nz - 1, 0.0, pltpu.roll(f, nz - 1, 1))

    def prev_z(f):
        return jnp.where(lanes(f.shape[0]) == 0, 0.0, pltpu.roll(f, 1, 1))

    def h_update(e, p, r, n, comps, keep=None):
        at, nxt = slice(r, r + n), slice(r + 1, r + n + 1)
        absorbs = flag[p, at] == 1
        hk = jnp.where(absorbs, hk1, 1.0)
        hg = jnp.where(absorbs, hg1, DT)
        ex, ey, ez = e[0, p, at], e[1, p, at], e[2, p, at]
        for c in comps:
            if c == 0:
                curl = (e[2, p, nxt] - ez) - (next_z(ey) - ey)
            elif c == 1:
                curl = (next_z(ex) - ex) - (e[2, p + 1, at] - ez)
            else:
                curl = (e[1, p + 1, at] - ey) - (e[0, p, nxt] - ex)
            new = hk * hf[c, p, at] - hg * curl
            if keep is not None:
                new = jnp.where(keep, new, 0.0)
            hf[c, p, at] = new

    tiles = ny // 8

    def h_inner(e):
        def body(p, carry):
            h_update(e, p, TOP, ny - 8, (0, 1, 2))
            return carry
        loop(1, nx, 4, body, 0)

    def h_outer(e):
        def body(p, carry):
            h_update(e, p, TOP + ny - 8, 8, (0, 1, 2))
            h_update(e, p, 0, 8, (0, 2), down)
            return carry
        h_update(e, 0, TOP, ny, (1, 2), left)
        h_update(e, nx, TOP, ny - 8, (0, 1, 2))
        loop(1, nx + 1, 4, body, 0)

    at = slice(TOP, TOP + ny)
    below = slice(TOP - 1, TOP + ny - 1)

    def e_update(step, src, dst, p, acc):
        hx, hy, hz = hf[0, p, at], hf[1, p, at], hf[2, p, at]
        keep, gain = ek[p - 1], eg[p - 1]
        curls = (
            lambda: (hz - hf[2, p, below]) - (hy - prev_z(hy)),
            lambda: (hx - prev_z(hx)) - (hz - hf[2, p - 1, at]),
            lambda: (hy - hf[1, p - 1, at]) - (hx - hf[0, p, below]),
        )
        for c in range(3):
            new = keep * src[c, p, at] + gain * curls[c]()
            dst[c, p, at] = new
            if c < 2:
                column = jnp.broadcast_to(new[:, nz // 2:nz // 2 + 1], (ny, nz))
                acc = jnp.where(lanes(ny) == (step * 2 + c) * nx + p - 1, column, acc)
        return acc

    loads[2].wait()
    loads[3].wait()

    def e_coefficients(p, carry):
        m = mat[p]
        absorbs = flag[p + 1, at] == 1
        k, g1, g0 = ek1[NMAT - 1], eg1[NMAT - 1], eg0[NMAT - 1]
        for i in range(NMAT - 2, -1, -1):
            here = m == i
            k = jnp.where(here, ek1[i], k)
            g1 = jnp.where(here, eg1[i], g1)
            g0 = jnp.where(here, eg0[i], g0)
        ek[p] = jnp.where(absorbs, k, 1.0)
        eg[p] = jnp.where(absorbs, g1, g0)
        return carry

    loop(0, nx, 4, e_coefficients, 0)
    loads[0].wait()
    loads[1].wait()
    h_inner(e0)
    wait_recv(round1)
    h_outer(e0)
    acc = jnp.zeros((ny, nz), jnp.float32)
    round2 = e_halo(e1, lambda x: x + 1, lambda y: y + TOP, e1, send2, recv2)
    for p in (1, nx):
        acc = e_update(0, e0, e1, p, acc)
    start(round2[0:2] + round2[4:6])
    acc = loop(2, nx, 4, functools.partial(e_update, 0, e0, e1), acc)
    start(round2[2:4])

    h_inner(e1)
    wait_recv(round2)
    h_outer(e1)
    stores = [
        pltpu.make_async_copy(hf.at[:, own_x, own_y], h_out, store_sem.at[0]),
        pltpu.make_async_copy(e0.at[:, own_x, own_y], e_out, store_sem.at[1]),
    ]
    stores[0].start()
    acc = loop(1, nx + 1, 4, functools.partial(e_update, 1, e1, e0), acc)
    mine = pl.ds(pl.multiple_of(gy * ny, ny), ny)
    samp[mine] = acc
    round3 = []
    for d in range(1, ngy):
        mate = lax.rem(gy + d, ngy)
        copy = pltpu.make_async_remote_copy(
            src_ref=samp.at[mine], dst_ref=samp.at[mine], send_sem=send3.at[d], recv_sem=recv3.at[d],
            device_id=(gx, mate), device_id_type=MESH)
        copy.start()
        round3.append(copy)
    stores[1].start()

    slots = spectra.shape[0]
    rows = lax.broadcasted_iota(jnp.int32, (8, nz), 0)
    angle = jnp.zeros((8, nz), jnp.float32)
    for n in range(STEPS):
        for k in range(slots):
            w = omega_in[lax.rem(gy * slots + k, NFREQ)]
            angle = jnp.where(rows == n * slots + k, w * ((n + 1) * DT), angle)
    cosine, sine = jnp.cos(angle), jnp.sin(angle)

    for copy in round3:
        copy.wait_recv()
    table = samp[...].T
    for k in range(slots):
        is_cos = gy * slots + k < NFREQ
        for c in range(2):
            total = None
            for n in range(STEPS):
                row = n * slots + k
                coef = jnp.where(is_cos, cosine[row:row + 1, 0:1], -sine[row:row + 1, 0:1])
                first = (n * 2 + c) * nx
                term = coef * table[first:first + nx]
                total = term if total is None else total + term
            spectra[k, c] = total

    wait_send(round1)
    wait_send(round2)
    for copy in round3:
        copy.wait_send()
    for copy in stores:
        copy.wait()


def solution(mesh):
    ngx, ngy = mesh.shape["gx"], mesh.shape["gy"]

    def local(electric, magnetic, material, pml_flags, permittivity, pml_sigma, omega):
        _, nx, ny, nz = electric.shape
        slots = 2 * NFREQ // ngy
        anywhere = pl.BlockSpec(memory_space=pl.ANY)
        scalars = pl.BlockSpec(memory_space=pltpu.SMEM)
        f32 = jnp.float32
        return pl.pallas_call(
            functools.partial(kernel, ngx, ngy, nx, ny, nz),
            out_shape=(
                jax.ShapeDtypeStruct(electric.shape, f32),
                jax.ShapeDtypeStruct(magnetic.shape, f32),
                jax.ShapeDtypeStruct((slots, 2, nx, ny * ngy), f32),
            ),
            in_specs=[anywhere] * 4 + [scalars, anywhere, scalars],
            out_specs=(anywhere, anywhere, pl.BlockSpec(memory_space=pltpu.VMEM)),
            scratch_shapes=[
                pltpu.VMEM((3, nx + 2, ny + 16, nz), f32),
                pltpu.VMEM((3, nx + 2, ny + 16, nz), f32),
                pltpu.VMEM((3, nx + 1, ny + 8, nz), f32),
                pltpu.VMEM((nx + 1, ny + 8, nz), jnp.int32),
                pltpu.VMEM((nx, ny, nz), jnp.int32),
                pltpu.VMEM((nx, ny, nz), f32),
                pltpu.VMEM((nx, ny, nz), f32),
                pltpu.SMEM((NMAT,), f32),
                pltpu.VMEM((1, nz), f32),
                pltpu.SMEM((NFREQ,), f32),
                pltpu.VMEM((ngy * ny, nz), f32),
                pltpu.SemaphoreType.DMA((5,)),
                pltpu.SemaphoreType.DMA((2,)),
                pltpu.SemaphoreType.DMA((12,)),
                pltpu.SemaphoreType.DMA((12,)),
                pltpu.SemaphoreType.DMA((7,)),
                pltpu.SemaphoreType.DMA((7,)),
                pltpu.SemaphoreType.DMA((ngy,)),
                pltpu.SemaphoreType.DMA((ngy,)),
            ],
            compiler_params=pltpu.CompilerParams(
                collective_id=0, has_side_effects=True, vmem_limit_bytes=24 * 1024 * 1024),
        )(electric, magnetic, material, pml_flags, permittivity, pml_sigma.reshape(1, nz), omega)

    placed = (
        P(None, "gx", "gy", None),
        P(None, "gx", "gy", None),
        P("gx", "gy", None),
        P("gx", "gy", None),
        P(),
        P(),
        P(),
    )
    return jax.shard_map(
        local,
        mesh=mesh,
        in_specs=placed,
        out_specs=(P(None, "gx", "gy", None), P(None, "gx", "gy", None), P("gy", None, "gx", None)),
        check_vma=False,
    )
```

time: 60.9 us -> 25.3 us (0.42)
  starting transfers between devices: 23.1 us -> 0 us
  Pallas kernels: 0 us -> 17.2 us
  other arithmetic: 8.49 us -> 0 us
  local copies, waits for them, and re-layouts: 15.7 us -> 7.24 us
  blocking collectives: 7.84 us -> 0 us
  waiting for transfers between devices: 3.74 us -> 0 us
  between operations: 1.41 us -> 0.67 us
    ppermute x8 -> x0, starting transfers between devices: 23.1 us -> none  [from_behind(): return lax.ppermute(x, axis, pairs)]
    pallas_call x0 -> x1, Pallas kernels: none -> 17.2 us  [local(): pl.pallas_call(functools.partial(kernel, ngx, ngy, nx, ny, nz), out_shape...]
    all_to_all x1 -> x0, blocking collectives: 7.84 us -> none  [local(): lax.all_to_all(partial_sums, 'gy', split_axis=0, concat_axis=3, tiled=True)]
    slice x28 -> x0, local copies, waits for them, and re-layouts: 6.92 us -> none  [the longest x4 2.8 us: local(): samples.append(electric[0:2, :, :, plane_at])]
    ppermute x8 -> x0, waiting for transfers between devices: 3.74 us -> none  [from_behind(): return lax.ppermute(x, axis, pairs)]
    div x1 -> x0, other arithmetic: 2.75 us -> none  [coefficients(): e_keep = (1.0 - s_ele) / (1.0 + s_ele)]
    sub x7 -> x0, other arithmetic: 2.69 us -> none  [the longest x2 1.92 us: forward_diff(): return jnp.concatenate([rest, rim], axis=axis) - field]
    another operation x8 -> x0, other arithmetic: 1.11 us -> none  [the longest x4 1.06 us: local(): jnp.stack([curl_x, curl_y, curl_z])]
  transfers between devices with their start and end apart: 8 -> 0, of which waited for: 4 -> 0; matrix products, arithmetic and copies ran while one was open for 12% -> 0% of each run, Pallas kernels for 0% -> 0%
where the time goes in v1:
time: 25.3 us; the launch traced here: 25.1 us
  Pallas kernels  17.2 us (68%)
  local copies, waits for them, and re-layouts  7.24 us (29%)
  between operations  0.67 us (3%)
    pallas_call x1, Pallas kernels, local(): pl.pallas_call(functools.partial(kernel, ngx, ngy, nx, ny, nz), out_shape...  17.2 us
    unnamed x17, local copies, waits for them, and re-layouts  7.24 us

profile of v1, /device:TPU:0, one launch (start us, length us, event | category | flops | bytes accessed | tf_op | source)
XLA Modules:
  0.0 25.1 jit_solution(9277017112198797683)
XLA Ops:
  0.6 0.0 copy-start.6
  0.6 0.0 copy-start.5
  0.7 0.0 copy-start.4
  0.7 0.6 %copy-done.6 = f32[8]{0:T(128)S(1)} copy-done((f32[8]{0:T(128)S(1)}, f32[8]{0:T(128)}, u32[]{:S(2)}) %copy-start.6) | copy-done | bytes 56
  1.3 0.0 copy-done.5
  1.3 0.0 copy-done.4
  1.3 0.0 copy-start
  1.3 1.1 %copy-done = f32[3,32,16,128]{3,2,1,0:T(8,128)S(1)} copy-done((f32[3,32,16,128]{3,2,1,0:T(8,128)S(1)}, f32[3,32,16,128]{3,2,1,0:T(8,128)}, u32[]{:S(2)}) %copy-start) | copy-done | bytes 786456
  2.5 0.0 copy-start.1
  2.5 1.1 %copy-done.1 = f32[3,32,16,128]{3,2,1,0:T(8,128)S(1)} copy-done((f32[3,32,16,128]{3,2,1,0:T(8,128)S(1)}, f32[3,32,16,128]{3,2,1,0:T(8,128)}, u32[]{:S(2)}) %copy-start.1) | copy-done | bytes 786456
  3.6 0.0 copy-start.2
  3.6 0.9 %copy-done.2 = s32[32,16,128]{2,1,0:T(8,128)S(1)} copy-done((s32[32,16,128]{2,1,0:T(8,128)S(1)}, s32[32,16,128]{2,1,0:T(8,128)}, u32[]{:S(2)}) %copy-start.2) | copy-done | bytes 262168
  4.5 0.0 copy-start.3
  4.5 0.9 %copy-done.3 = s32[32,16,128]{2,1,0:T(8,128)S(1)} copy-done((s32[32,16,128]{2,1,0:T(8,128)S(1)}, s32[32,16,128]{2,1,0:T(8,128)}, u32[]{:S(2)}) %copy-start.3) | copy-done | bytes 262168
  5.5 17.2 %shard_map.94 = (f32[3,32,16,128]{3,2,1,0:T(8,128)S(1)}, f32[3,32,16,128]{3,2,1,0:T(8,128)S(1)}, f32[4,2,32,64]{3,2,1,0:T(8,128)S(1)}) custom-call(f32[3,32,16,128]{3,2,1,0:T(8,128)S(1)} %copy-done, f32[3,32,16,128]{3,2,1,0:T(8,128)S(1)} %copy-done.1, s32[32,16,128]{2,1,0:T(8,128)S(1)} %copy-done.2, s32[32,16,128]{2,1,0:T(8,128)S(1)} %copy-done.3, ...), custom_call_target="tpu_custom_call" | custom-call | tf_op jit(solution)/shard_map/pallas_call | solution.py:314
  22.7 0.9 %copy.13 = f32[3,32,16,128]{3,2,1,0:T(8,128)} copy(f32[3,32,16,128]{3,2,1,0:T(8,128)S(1)} %get-tuple-element.6) | data formatting | bytes 1572864
  23.5 0.9 %copy.14 = f32[3,32,16,128]{3,2,1,0:T(8,128)} copy(f32[3,32,16,128]{3,2,1,0:T(8,128)S(1)} %get-tuple-element.7) | data formatting | bytes 1572864
  24.4 0.7 %copy.15 = f32[4,2,32,64]{3,2,1,0:T(8,128)} copy(f32[4,2,32,64]{3,2,1,0:T(8,128)S(1)} %get-tuple-element.8) | data formatting | bytes 131072
Async XLA Ops:
  0.6 0.7 %copy-start.6 = (f32[8]{0:T(128)S(1)}, f32[8]{0:T(128)}, u32[]{:S(2)}) copy-start(f32[8]{0:T(128)} %omega_in.1) | copy-start | bytes 100
  0.6 0.7 %copy-start.5 = (f32[128]{0:T(128)S(1)}, f32[128]{0:T(128)}, u32[]{:S(2)}) copy-start(f32[128]{0:T(128)} %param.12) | copy-start | bytes 1540
  0.7 0.7 %copy-start.4 = (f32[4]{0:T(128)S(1)}, f32[4]{0:T(128)}, u32[]{:S(2)}) copy-start(f32[4]{0:T(128)} %perm_in.1) | copy-start | bytes 52
  1.3 1.1 %copy-start = (f32[3,32,16,128]{3,2,1,0:T(8,128)S(1)}, f32[3,32,16,128]{3,2,1,0:T(8,128)}, u32[]{:S(2)}) copy-start(f32[3,32,16,128]{3,2,1,0:T(8,128)} %e_in.1) | copy-start | bytes 2359300
  2.5 1.1 %copy-start.1 = (f32[3,32,16,128]{3,2,1,0:T(8,128)S(1)}, f32[3,32,16,128]{3,2,1,0:T(8,128)}, u32[]{:S(2)}) copy-start(f32[3,32,16,128]{3,2,1,0:T(8,128)} %h_in.1) | copy-start | bytes 2359300
  3.6 0.9 %copy-start.2 = (s32[32,16,128]{2,1,0:T(8,128)S(1)}, s32[32,16,128]{2,1,0:T(8,128)}, u32[]{:S(2)}) copy-start(s32[32,16,128]{2,1,0:T(8,128)} %mat_in.1) | copy-start | bytes 786436
  4.5 0.9 %copy-start.3 = (s32[32,16,128]{2,1,0:T(8,128)S(1)}, s32[32,16,128]{2,1,0:T(8,128)}, u32[]{:S(2)}) copy-start(s32[32,16,128]{2,1,0:T(8,128)} %flag_in.1) | copy-start | bytes 786436

commit v2 on v1

v2 whole, which is shorter than its diff:
```python
import functools

import jax
import jax.numpy as jnp
from jax import lax
from jax.experimental import pallas as pl
from jax.experimental.pallas import tpu as pltpu
from jax.sharding import PartitionSpec as P

STEPS = 2
NFREQ = 8
NMAT = 4
DT = 0.5
MESH = pl.DeviceIdType.MESH

TOP = 8


BLOCK = 8


def blocks(low, high, body, carry=0):
    return lax.fori_loop(0, (high - low) // BLOCK, lambda i, c: body(low + i * BLOCK, c), carry)


def kernel(ngx, ngy, nx, ny, nz,
           e_in, h_in, mat_in, flag_in, perm_in, sigma_in, omega_in,
           e_out, h_out, samp, weights,
           e0, e1, h0, h1, h2, flag, mat, ek, eg, perm, sigma, omega,
           load_sem, send1, recv1, send2, recv2, send3, recv3):
    gx, gy = lax.axis_index("gx"), lax.axis_index("gy")
    left, right = gx > 0, gx < ngx - 1
    down, up = gy > 0, gy < ngy - 1
    own_x = pl.ds(1, nx)
    own_y = pl.ds(TOP, ny)
    behind, ahead = TOP - 1, TOP + ny
    last = nx + 1

    loads = [
        pltpu.make_async_copy(e_in, e0.at[:, own_x, own_y], load_sem.at[0]),
        pltpu.make_async_copy(h_in, h0.at[:, own_x, own_y], load_sem.at[1]),
        pltpu.make_async_copy(flag_in, flag.at[own_x, own_y], load_sem.at[2]),
        pltpu.make_async_copy(mat_in, mat, load_sem.at[3]),
        pltpu.make_async_copy(sigma_in, sigma, load_sem.at[4]),
        pltpu.make_async_copy(perm_in, perm, load_sem.at[5]),
        pltpu.make_async_copy(omega_in, omega, load_sem.at[6]),
    ]
    for copy in loads:
        copy.start()

    barrier = pltpu.get_barrier_semaphore()
    partners = [
        (left, (gx - 1, gy)),
        (right, (gx + 1, gy)),
        (left & up, (gx - 1, gy + 1)),
        (right & down, (gx + 1, gy - 1)),
    ]
    expected = ngy - 1
    for there, device in partners:
        expected = expected + there.astype(jnp.int32)

        @pl.when(there)
        def _():
            pl.semaphore_signal(barrier, inc=1, device_id=device, device_id_type=MESH)

    for d in range(1, ngy):
        pl.semaphore_signal(barrier, inc=1, device_id=(gx, lax.rem(gy + d, ngy)), device_id_type=MESH)

    @pl.when(jnp.logical_not(right))
    def _():
        for e in (e0, e1):
            for c in (1, 2):
                e[c, last, 0:ahead] = jnp.zeros((ahead, nz), jnp.float32)

    @pl.when(jnp.logical_not(up))
    def _():
        for e in (e0, e1):
            for c in (0, 2):
                e[c, 0:last, ahead:ahead + 8] = jnp.zeros((last, 8, nz), jnp.float32)

    pl.semaphore_wait(barrier, expected)

    def remote(src, dst, sends, recvs, i, device):
        return pltpu.make_async_remote_copy(
            src_ref=src, dst_ref=dst, send_sem=sends.at[i], recv_sem=recvs.at[i],
            device_id=device, device_id_type=MESH)

    def e_halo(src, x_of, y_of, e, sends, recvs):
        at = functools.partial(remote, sends=sends, recvs=recvs)
        xs = pl.ds(x_of(0), nx)
        ys = pl.ds(y_of(0), ny)
        to_left = [at(src.at[1:3, x_of(0), ys], e.at[1:3, last, own_y], i=0, device=(gx - 1, gy))]
        to_right = [at(src.at[:, x_of(nx - 1), ys], e.at[:, 0, own_y], i=1, device=(gx + 1, gy))]
        to_down = [at(src.at[c, xs, y_of(0)], e.at[c, own_x, ahead], i=2 + c // 2, device=(gx, gy - 1)) for c in (0, 2)]
        to_up = [at(src.at[:, xs, y_of(ny - 1)], e.at[:, own_x, behind], i=4, device=(gx, gy + 1))]
        corner_lu = [at(src.at[1, x_of(0), y_of(ny - 1)], e.at[1, last, behind], i=5, device=(gx - 1, gy + 1))]
        corner_rd = [at(src.at[0, x_of(nx - 1), y_of(0)], e.at[0, 0, ahead], i=6, device=(gx + 1, gy - 1))]
        return [
            [left, right, to_left],
            [right, left, to_right],
            [down, up, to_down],
            [up, down, to_up],
            [left & up, right & down, corner_lu],
            [right & down, left & up, corner_rd],
        ]

    def start(plan):
        for sends, _, copies in plan:
            @pl.when(sends)
            def _():
                for copy in copies:
                    copy.start()

    def wait_recv(plan):
        for _, receives, copies in plan:
            @pl.when(receives)
            def _():
                for copy in copies:
                    copy.wait_recv()

    def wait_send(plan):
        for sends, _, copies in plan:
            @pl.when(sends)
            def _():
                for copy in copies:
                    copy.wait_send()

    round1 = e_halo(e_in, lambda x: x, lambda y: y, e0, send1, recv1)
    at1 = functools.partial(remote, sends=send1, recvs=recv1)
    round1[1][2] += [
        at1(h_in.at[1:3, nx - 1], h0.at[1:3, 0, own_y], i=7, device=(gx + 1, gy)),
        at1(flag_in.at[nx - 1], flag.at[0, own_y], i=8, device=(gx + 1, gy)),
    ]
    round1[3][2] += [
        at1(h_in.at[0, :, ny - 1], h0.at[0, own_x, behind], i=9, device=(gx, gy + 1)),
        at1(h_in.at[2, :, ny - 1], h0.at[2, own_x, behind], i=10, device=(gx, gy + 1)),
        at1(flag_in.at[:, ny - 1], flag.at[own_x, behind], i=11, device=(gx, gy + 1)),
    ]
    start(round1)

    loads[4].wait()
    loads[5].wait()
    sg = sigma[...]
    sm = sg * DT / 2.0
    hk1 = (1.0 - sm) / (1.0 + sm)
    hg1 = DT / (1.0 + sm)
    ek1, eg1, eg0 = [], [], []
    for m in range(NMAT):
        eps = jnp.full((1, nz), perm[m], jnp.float32)
        se = sg * DT / (2.0 * eps)
        ek1.append((1.0 - se) / (1.0 + se))
        eg1.append(DT / (eps * (1.0 + se)))
        eg0.append(DT / eps)

    def lanes(f):
        return lax.broadcasted_iota(jnp.int32, f.shape, f.ndim - 1)

    def next_z(f):
        return jnp.where(lanes(f) == nz - 1, 0.0, pltpu.roll(f, nz - 1, f.ndim - 1))

    def prev_z(f):
        return jnp.where(lanes(f) == 0, 0.0, pltpu.roll(f, 1, f.ndim - 1))

    def h_update(e, src, dst, p, planes, r, n, comps, keep=None):
        at, nxt = slice(r, r + n), slice(r + 1, r + n + 1)
        ps, ahead_x = pl.ds(p, planes), pl.ds(p + 1, planes)
        absorbs = flag[ps, at] == 1
        hk = jnp.where(absorbs, hk1, 1.0)
        hg = jnp.where(absorbs, hg1, DT)
        ex, ey, ez = e[0, ps, at], e[1, ps, at], e[2, ps, at]
        curls = (
            lambda: (e[2, ps, nxt] - ez) - (next_z(ey) - ey),
            lambda: (next_z(ex) - ex) - (e[2, ahead_x, at] - ez),
            lambda: (e[1, ahead_x, at] - ey) - (e[0, ps, nxt] - ex),
        )
        results = []
        for c in comps:
            new = hk * src[c, ps, at] - hg * curls[c]()
            results.append(new if keep is None else jnp.where(keep, new, 0.0))
        for c, new in zip(comps, results):
            dst[c, ps, at] = new

    low, high = TOP, TOP + ny
    inner_end = 1 + (nx - 1) // BLOCK * BLOCK

    def h_inner(e, src, dst):
        def body(p, carry):
            h_update(e, src, dst, p, BLOCK, low, ny - 8, (0, 1, 2))
            return carry
        blocks(1, inner_end, body)

    def h_outer(e, src, dst):
        def body(p, carry):
            h_update(e, src, dst, p, BLOCK, high - 8, 8, (0, 1, 2))
            h_update(e, src, dst, p, BLOCK, 0, 8, (0, 2), down)
            return carry
        h_update(e, src, dst, 0, 1, low, ny, (1, 2), left)
        h_update(e, src, dst, inner_end, nx + 1 - inner_end, low, ny - 8, (0, 1, 2))
        blocks(1, nx + 1, body)

    def e_update(step, src, h, dst, dst_x, dst_y, p, acc):
        for r in range(0, ny, 8):
            at, below = slice(low + r, low + r + 8), slice(low + r - 1, low + r + 7)
            ps, behind_x = pl.ds(p, BLOCK), pl.ds(p - 1, BLOCK)
            hx, hy, hz = h[0, ps, at], h[1, ps, at], h[2, ps, at]
            keep, gain = ek[behind_x, r:r + 8], eg[behind_x, r:r + 8]
            curls = (
                lambda: (hz - h[2, ps, below]) - (hy - prev_z(hy)),
                lambda: (hx - prev_z(hx)) - (hz - h[2, behind_x, at]),
                lambda: (hy - h[1, behind_x, at]) - (hx - h[0, ps, below]),
            )
            news = [keep * src[c, ps, at] + gain * curls[c]() for c in range(3)]
            for c in range(3):
                dst[c, pl.ds(p + dst_x, BLOCK), r + dst_y:r + dst_y + 8] = news[c]
            piece = acc[r // 8]
            for c in range(2):
                for k in range(BLOCK):
                    column = jnp.broadcast_to(news[c][k, :, nz // 2:nz // 2 + 1], (8, nz))
                    piece = jnp.where(lanes(piece) == (step * 2 + c) * nx + p - 1 + k, column, piece)
            acc = acc[:r // 8] + (piece,) + acc[r // 8 + 1:]
        return acc

    loads[2].wait()
    loads[3].wait()

    def e_coefficients(p, carry):
        ps = pl.ds(p, BLOCK)
        m = mat[ps]
        absorbs = flag[pl.ds(p + 1, BLOCK), low:high] == 1
        k, g1, g0 = ek1[NMAT - 1], eg1[NMAT - 1], eg0[NMAT - 1]
        for i in range(NMAT - 2, -1, -1):
            here = m == i
            k = jnp.where(here, ek1[i], k)
            g1 = jnp.where(here, eg1[i], g1)
            g0 = jnp.where(here, eg0[i], g0)
        ek[ps] = jnp.where(absorbs, k, 1.0)
        eg[ps] = jnp.where(absorbs, g1, g0)
        return carry

    blocks(0, nx, e_coefficients)
    loads[0].wait()
    loads[1].wait()
    h_inner(e0, h0, h1)
    wait_recv(round1)
    h_outer(e0, h0, h1)
    acc = tuple(jnp.zeros((8, nz), jnp.float32) for _ in range(ny // 8))
    step1 = functools.partial(e_update, 0, e0, h1, e1, 0, TOP)
    round2 = e_halo(e1, lambda x: x + 1, lambda y: y + TOP, e1, send2, recv2)
    acc = step1(1, acc)
    acc = step1(nx + 1 - BLOCK, acc)
    start(round2[0:2] + round2[4:6])
    acc = blocks(1 + BLOCK, nx + 1 - BLOCK, step1, acc)
    start(round2[2:4])

    h_inner(e1, h1, h2)
    wait_recv(round2)
    h_outer(e1, h1, h2)
    acc = blocks(1, nx + 1, functools.partial(e_update, 1, e1, h2, e_out, -1, 0), acc)
    mine = pl.ds(pl.multiple_of(gy * ny, ny), ny)
    samp[mine] = jnp.concatenate(acc, axis=0)
    round3 = []
    for d in range(1, ngy):
        mate = lax.rem(gy + d, ngy)
        copy = pltpu.make_async_remote_copy(
            src_ref=samp.at[mine], dst_ref=samp.at[mine], send_sem=send3.at[d], recv_sem=recv3.at[d],
            device_id=(gx, mate), device_id_type=MESH)
        copy.start()
        round3.append(copy)
    h_out[...] = h2[:, 1:nx + 1, low:high]
    loads[6].wait()
    slots = 2 * NFREQ // ngy
    rows = lax.broadcasted_iota(jnp.int32, (8, nz), 0)
    angle = jnp.zeros((8, nz), jnp.float32)
    is_cos = jnp.zeros((8, nz), jnp.bool_)
    for n in range(STEPS):
        for k in range(slots):
            here = rows == n * slots + k
            slot = gy * slots + k
            angle = jnp.where(here, omega[lax.rem(slot, NFREQ)] * ((n + 1) * DT), angle)
            is_cos = is_cos | (here & (slot < NFREQ))
    weights[...] = jnp.where(is_cos, jnp.cos(angle), -jnp.sin(angle))
    wait_send(round1)
    wait_send(round2)
    for copy in round3:
        copy.wait_recv()
    for copy in round3:
        copy.wait_send()


def finish(nx, e_in, h_in, samp, weights, e_out, h_out, spectra_out, spectra, sems):
    copies = [
        pltpu.make_async_copy(e_in, e_out, sems.at[0]),
        pltpu.make_async_copy(h_in, h_out, sems.at[1]),
        pltpu.make_async_copy(spectra, spectra_out, sems.at[2]),
    ]
    copies[0].start()
    copies[1].start()
    slots = spectra.shape[0]
    table = samp[...].T
    for k in range(slots):
        for c in range(2):
            total = None
            for n in range(STEPS):
                row = n * slots + k
                coef = weights[row:row + 1, 0:1]
                first = (n * 2 + c) * nx
                term = coef * table[first:first + nx]
                total = term if total is None else total + term
            spectra[k, c] = total
    copies[2].start()
    for copy in copies:
        copy.wait()


def solution(mesh):
    ngx, ngy = mesh.shape["gx"], mesh.shape["gy"]

    def local(electric, magnetic, material, pml_flags, permittivity, pml_sigma, omega):
        _, nx, ny, nz = electric.shape
        slots = 2 * NFREQ // ngy
        hbm = pl.BlockSpec(memory_space=pltpu.HBM)
        vmem = pl.BlockSpec(memory_space=pltpu.VMEM)
        f32 = jnp.float32
        field = jax.ShapeDtypeStruct(electric.shape, f32)
        e_scratch = pltpu.VMEM((3, nx + 2, ny + 16, nz), f32)
        h_scratch = pltpu.VMEM((3, nx + 1, ny + 8, nz), f32)
        operands = (electric, magnetic, material, pml_flags, permittivity, pml_sigma.reshape(1, nz), omega)
        e_done, h_done, samples, weights = pl.pallas_call(
            functools.partial(kernel, ngx, ngy, nx, ny, nz),
            out_shape=(
                pltpu.VMEM(field.shape, f32),
                pltpu.VMEM(field.shape, f32),
                pltpu.VMEM((ngy * ny, nz), f32),
                pltpu.VMEM((8, nz), f32),
            ),
            in_specs=[hbm] * 7,
            out_specs=(vmem, vmem, vmem, vmem),
            scratch_shapes=[
                e_scratch,
                e_scratch,
                h_scratch,
                h_scratch,
                h_scratch,
                pltpu.VMEM((nx + 1, ny + 8, nz), jnp.int32),
                pltpu.VMEM((nx, ny, nz), jnp.int32),
                pltpu.VMEM((nx, ny, nz), f32),
                pltpu.VMEM((nx, ny, nz), f32),
                pltpu.SMEM((NMAT,), f32),
                pltpu.VMEM((1, nz), f32),
                pltpu.SMEM((NFREQ,), f32),
                pltpu.SemaphoreType.DMA((7,)),
                pltpu.SemaphoreType.DMA((12,)),
                pltpu.SemaphoreType.DMA((12,)),
                pltpu.SemaphoreType.DMA((7,)),
                pltpu.SemaphoreType.DMA((7,)),
                pltpu.SemaphoreType.DMA((ngy,)),
                pltpu.SemaphoreType.DMA((ngy,)),
            ],
            compiler_params=pltpu.CompilerParams(
                collective_id=0, has_side_effects=True, vmem_limit_bytes=24 * 1024 * 1024),
        )(*[pltpu.with_memory_space_constraint(a, pltpu.HBM) for a in operands])
        spectra = jax.ShapeDtypeStruct((slots, 2, nx, ny * ngy), f32)
        return pl.pallas_call(
            functools.partial(finish, nx),
            out_shape=(field, field, spectra),
            in_specs=[vmem] * 4,
            out_specs=(hbm, hbm, hbm),
            scratch_shapes=[pltpu.VMEM(spectra.shape, f32), pltpu.SemaphoreType.DMA((3,))],
            compiler_params=pltpu.CompilerParams(vmem_limit_bytes=24 * 1024 * 1024),
        )(e_done, h_done, samples, weights)

    placed = (
        P(None, "gx", "gy", None),
        P(None, "gx", "gy", None),
        P("gx", "gy", None),
        P("gx", "gy", None),
        P(),
        P(),
        P(),
    )
    return jax.shard_map(
        local,
        mesh=mesh,
        in_specs=placed,
        out_specs=(P(None, "gx", "gy", None), P(None, "gx", "gy", None), P("gy", None, "gx", None)),
        check_vma=False,
    )
```

time: 25.3 us -> 17.5 us (0.69)
  local copies, waits for them, and re-layouts: 7.24 us -> 0 us
  Pallas kernels: 17.2 us -> 16.8 us
    unnamed x17 -> x0, local copies, waits for them, and re-layouts: 7.24 us -> none
    pallas_call x1, Pallas kernels: 17.2 us -> 15.6 us  [local(): pl.pallas_call(functools.partial(kernel, ngx, ngy, nx, ny, nz), out_shape...]
    pallas_call x0 -> x1, Pallas kernels: none -> 1.2 us  [local(): pl.pallas_call(functools.partial(finish, nx), out_shape=(field, field, sp...]
where the time goes in v2:
time: 17.5 us; the launch traced here: 17.4 us
  Pallas kernels  16.8 us (96%)
  between operations  0.64 us (4%)
    pallas_call x1, Pallas kernels, local(): pl.pallas_call(functools.partial(kernel, ngx, ngy, nx, ny, nz), out_shape...  15.6 us
    pallas_call x1, Pallas kernels, local(): pl.pallas_call(functools.partial(finish, nx), out_shape=(field, field, sp...  1.2 us

profile of v2, /device:TPU:0, one launch (start us, length us, event | category | flops | bytes accessed | tf_op | source)
XLA Modules:
  0.0 17.4 jit_solution(5887893077824999483)
XLA Ops:
  0.6 15.6 %shard_map.94 = (f32[3,32,16,128]{3,2,1,0:T(8,128)S(1)}, f32[3,32,16,128]{3,2,1,0:T(8,128)S(1)}, f32[64,128]{1,0:T(8,128)S(1)}, f32[8,128]{1,0:T(8,128)S(1)}) custom-call(f32[3,32,16,128]{3,2,1,0:T(8,128)} %e_in.1, f32[3,32,16,128]{3,2,1,0:T(8,128)} %h_in.1, s32[32,16,128]{2,1,0:T(8,128)} %mat_in.1, s32[32,16,128]{2,1,0:T(8,128)} %flag_in.1, f32[4]{0:T(128)} %perm_in.1, ...), custom_call_target="tpu_custom_call" | custom-call | tf_op jit(solution)/shard_map/pallas_call | solution.py:328
  16.2 1.2 %shard_map.95 = (f32[3,32,16,128]{3,2,1,0:T(8,128)}, f32[3,32,16,128]{3,2,1,0:T(8,128)}, f32[4,2,32,64]{3,2,1,0:T(8,128)}) custom-call(f32[3,32,16,128]{3,2,1,0:T(8,128)S(1)} %get-tuple-element.7.e_in, f32[3,32,16,128]{3,2,1,0:T(8,128)S(1)} %get-tuple-element.8.h_in, f32[64,128]{1,0:T(8,128)S(1)} %get-tuple-element.9.samp, ...), custom_call_target="tpu_custom_call" | custom-call | tf_op jit(solution)/shard_map/pallas_call | solution.py:363

commit v3 on v2

--- a/solution.py
+++ b/solution.py
@@ -20,7 +20,9 @@
 
 
 def blocks(low, high, body, carry=0):
-    return lax.fori_loop(0, (high - low) // BLOCK, lambda i, c: body(low + i * BLOCK, c), carry)
+    for p in range(low, high, BLOCK):
+        carry = body(p, carry)
+    return carry
 
 
 def kernel(ngx, ngy, nx, ny, nz,
@@ -198,7 +200,7 @@
         h_update(e, src, dst, inner_end, nx + 1 - inner_end, low, ny - 8, (0, 1, 2))
         blocks(1, nx + 1, body)
 
-    def e_update(step, src, h, dst, dst_x, dst_y, p, acc):
+    def e_update(step, src, h, dst, dst_x, dst_y, comps, p, acc):
         for r in range(0, ny, 8):
             at, below = slice(low + r, low + r + 8), slice(low + r - 1, low + r + 7)
             ps, behind_x = pl.ds(p, BLOCK), pl.ds(p - 1, BLOCK)
@@ -209,11 +211,11 @@
                 lambda: (hx - prev_z(hx)) - (hz - h[2, behind_x, at]),
                 lambda: (hy - h[1, behind_x, at]) - (hx - h[0, ps, below]),
             )
-            news = [keep * src[c, ps, at] + gain * curls[c]() for c in range(3)]
-            for c in range(3):
+            news = {c: keep * src[c, ps, at] + gain * curls[c]() for c in comps}
+            for c in comps:
                 dst[c, pl.ds(p + dst_x, BLOCK), r + dst_y:r + dst_y + 8] = news[c]
             piece = acc[r // 8]
-            for c in range(2):
+            for c in (c for c in comps if c < 2):
                 for k in range(BLOCK):
                     column = jnp.broadcast_to(news[c][k, :, nz // 2:nz // 2 + 1], (8, nz))
                     piece = jnp.where(lanes(piece) == (step * 2 + c) * nx + p - 1 + k, column, piece)
@@ -244,7 +246,7 @@
     wait_recv(round1)
     h_outer(e0, h0, h1)
     acc = tuple(jnp.zeros((8, nz), jnp.float32) for _ in range(ny // 8))
-    step1 = functools.partial(e_update, 0, e0, h1, e1, 0, TOP)
+    step1 = functools.partial(e_update, 0, e0, h1, e1, 0, TOP, (0, 1, 2))
     round2 = e_halo(e1, lambda x: x + 1, lambda y: y + TOP, e1, send2, recv2)
     acc = step1(1, acc)
     acc = step1(nx + 1 - BLOCK, acc)
@@ -255,7 +257,8 @@
     h_inner(e1, h1, h2)
     wait_recv(round2)
     h_outer(e1, h1, h2)
-    acc = blocks(1, nx + 1, functools.partial(e_update, 1, e1, h2, e_out, -1, 0), acc)
+    step2 = functools.partial(e_update, 1, e1, h2, e_out, -1, 0)
+    acc = blocks(1, nx + 1, functools.partial(step2, (0, 1)), acc)
     mine = pl.ds(pl.multiple_of(gy * ny, ny), ny)
     samp[mine] = jnp.concatenate(acc, axis=0)
     round3 = []
@@ -266,6 +269,7 @@
             device_id=(gx, mate), device_id_type=MESH)
         copy.start()
         round3.append(copy)
+    blocks(1, nx + 1, functools.partial(step2, (2,)), acc)
     h_out[...] = h2[:, 1:nx + 1, low:high]
     loads[6].wait()
     slots = 2 * NFREQ // ngy

time: 17.5 us -> 17.1 us (0.977)
  Pallas kernels: 16.8 us -> 16.3 us
    pallas_call x1, Pallas kernels: 15.6 us -> 15.1 us  [local(): pl.pallas_call(functools.partial(kernel, ngx, ngy, nx, ny, nz), out_shape...]
where the time goes in v3:
time: 17.1 us; the launch traced here: 16.9 us
  Pallas kernels  16.3 us (95%)
  between operations  0.64 us (4%)
    pallas_call x1, Pallas kernels, local(): pl.pallas_call(functools.partial(kernel, ngx, ngy, nx, ny, nz), out_shape...  15.1 us
    pallas_call x1, Pallas kernels, local(): pl.pallas_call(functools.partial(finish, nx), out_shape=(field, field, sp...  1.2 us

profile of v3, /device:TPU:0, one launch (start us, length us, event | category | flops | bytes accessed | tf_op | source)
XLA Modules:
  0.0 16.9 jit_solution(18116107407211253563)
XLA Ops:
  0.6 15.1 %shard_map.94 = (f32[3,32,16,128]{3,2,1,0:T(8,128)S(1)}, f32[3,32,16,128]{3,2,1,0:T(8,128)S(1)}, f32[64,128]{1,0:T(8,128)S(1)}, f32[8,128]{1,0:T(8,128)S(1)}) custom-call(f32[3,32,16,128]{3,2,1,0:T(8,128)} %e_in.1, f32[3,32,16,128]{3,2,1,0:T(8,128)} %h_in.1, s32[32,16,128]{2,1,0:T(8,128)} %mat_in.1, s32[32,16,128]{2,1,0:T(8,128)} %flag_in.1, f32[4]{0:T(128)} %perm_in.1, ...), custom_call_target="tpu_custom_call" | custom-call | tf_op jit(solution)/shard_map/pallas_call | solution.py:332
  15.7 1.2 %shard_map.95 = (f32[3,32,16,128]{3,2,1,0:T(8,128)}, f32[3,32,16,128]{3,2,1,0:T(8,128)}, f32[4,2,32,64]{3,2,1,0:T(8,128)}) custom-call(f32[3,32,16,128]{3,2,1,0:T(8,128)S(1)} %get-tuple-element.7.e_in, f32[3,32,16,128]{3,2,1,0:T(8,128)S(1)} %get-tuple-element.8.h_in, f32[64,128]{1,0:T(8,128)S(1)} %get-tuple-element.9.samp, ...), custom_call_target="tpu_custom_call" | custom-call | tf_op jit(solution)/shard_map/pallas_call | solution.py:367

commit v4 on v3

--- a/solution.py
+++ b/solution.py
@@ -16,7 +16,7 @@
 TOP = 8
 
 
-BLOCK = 8
+BLOCK = 4
 
 
 def blocks(low, high, body, carry=0):
@@ -28,7 +28,7 @@
 def kernel(ngx, ngy, nx, ny, nz,
            e_in, h_in, mat_in, flag_in, perm_in, sigma_in, omega_in,
            e_out, h_out, samp, weights,
-           e0, e1, h0, h1, h2, flag, mat, ek, eg, perm, sigma, omega,
+           e0, e1, h0, h1, h2, down0, down1, up0, up1, above0, above1, below0, below1, rim_h, rim_flag_out, rim_flag, flag, mat, ek, eg, perm, sigma, omega,
            load_sem, send1, recv1, send2, recv2, send3, recv3):
     gx, gy = lax.axis_index("gx"), lax.axis_index("gy")
     left, right = gx > 0, gx < ngx - 1
@@ -76,9 +76,39 @@
 
     @pl.when(jnp.logical_not(up))
     def _():
-        for e in (e0, e1):
-            for c in (0, 2):
-                e[c, 0:last, ahead:ahead + 8] = jnp.zeros((last, 8, nz), jnp.float32)
+        for e, above in ((e0, above0), (e1, above1)):
+            e[0, 0, ahead:ahead + 8] = jnp.zeros((8, nz), jnp.float32)
+            above[...] = jnp.zeros((2, nx, nz), jnp.float32)
+
+    for e in (e0, e1):
+        for c in (0, 2):
+            e[c, 1:last, ahead:ahead + 8] = jnp.zeros((nx, 8, nz), jnp.float32)
+
+    def row_of(ref, c, first, r):
+        planes, rows = ref.shape[-3], ref.shape[-2]
+        return pl.ds((c * planes + first) * rows + r, nx, stride=rows)
+
+    def get_rows(ref, c, first, r):
+        return ref.reshape(-1, nz)[row_of(ref, c, first, r), :]
+
+    def put_rows(ref, c, first, r, value):
+        ref.reshape(-1, nz)[row_of(ref, c, first, r), :] = value
+
+    def pack_down(e, down_rows):
+        for i, c in enumerate((0, 2)):
+            down_rows[i] = get_rows(e, c, 1, TOP)
+
+    def pack_up(e, up_rows):
+        for c in range(3):
+            up_rows[c] = get_rows(e, c, 1, TOP + ny - 1)
+
+    for i in (0, 1, 2):
+        loads[i].wait()
+    pack_down(e0, down0)
+    pack_up(e0, up0)
+    for i, c in enumerate((0, 2)):
+        up0[3 + i] = get_rows(h0, c, 1, TOP + ny - 1)
+    rim_flag_out[...] = get_rows(flag, 0, 1, TOP + ny - 1)
 
     pl.semaphore_wait(barrier, expected)
 
@@ -87,16 +117,15 @@
             src_ref=src, dst_ref=dst, send_sem=sends.at[i], recv_sem=recvs.at[i],
             device_id=device, device_id_type=MESH)
 
-    def e_halo(src, x_of, y_of, e, sends, recvs):
+    def e_halo(e, down_rows, up_rows, above, below, sends, recvs):
         at = functools.partial(remote, sends=sends, recvs=recvs)
-        xs = pl.ds(x_of(0), nx)
-        ys = pl.ds(y_of(0), ny)
-        to_left = [at(src.at[1:3, x_of(0), ys], e.at[1:3, last, own_y], i=0, device=(gx - 1, gy))]
-        to_right = [at(src.at[:, x_of(nx - 1), ys], e.at[:, 0, own_y], i=1, device=(gx + 1, gy))]
-        to_down = [at(src.at[c, xs, y_of(0)], e.at[c, own_x, ahead], i=2 + c // 2, device=(gx, gy - 1)) for c in (0, 2)]
-        to_up = [at(src.at[:, xs, y_of(ny - 1)], e.at[:, own_x, behind], i=4, device=(gx, gy + 1))]
-        corner_lu = [at(src.at[1, x_of(0), y_of(ny - 1)], e.at[1, last, behind], i=5, device=(gx - 1, gy + 1))]
-        corner_rd = [at(src.at[0, x_of(nx - 1), y_of(0)], e.at[0, 0, ahead], i=6, device=(gx + 1, gy - 1))]
+        rim_up = TOP + ny - 1
+        to_left = [at(e.at[1:3, 1, own_y], e.at[1:3, last, own_y], i=0, device=(gx - 1, gy))]
+        to_right = [at(e.at[:, nx, own_y], e.at[:, 0, own_y], i=1, device=(gx + 1, gy))]
+        to_down = [at(down_rows, above, i=2, device=(gx, gy - 1))]
+        to_up = [at(up_rows, below.at[:, 0:nx], i=3, device=(gx, gy + 1))]
+        corner_lu = [at(e.at[1, 1, rim_up], e.at[1, last, behind], i=4, device=(gx - 1, gy + 1))]
+        corner_rd = [at(e.at[0, nx, TOP], e.at[0, 0, ahead], i=5, device=(gx + 1, gy - 1))]
         return [
             [left, right, to_left],
             [right, left, to_right],
@@ -127,17 +156,13 @@
                 for copy in copies:
                     copy.wait_send()
 
-    round1 = e_halo(e_in, lambda x: x, lambda y: y, e0, send1, recv1)
+    round1 = e_halo(e0, down0, up0, above0, below0, send1, recv1)
     at1 = functools.partial(remote, sends=send1, recvs=recv1)
     round1[1][2] += [
-        at1(h_in.at[1:3, nx - 1], h0.at[1:3, 0, own_y], i=7, device=(gx + 1, gy)),
-        at1(flag_in.at[nx - 1], flag.at[0, own_y], i=8, device=(gx + 1, gy)),
+        at1(h0.at[1:3, nx, own_y], h0.at[1:3, 0, own_y], i=6, device=(gx + 1, gy)),
+        at1(flag.at[nx, own_y], flag.at[0, own_y], i=7, device=(gx + 1, gy)),
     ]
-    round1[3][2] += [
-        at1(h_in.at[0, :, ny - 1], h0.at[0, own_x, behind], i=9, device=(gx, gy + 1)),
-        at1(h_in.at[2, :, ny - 1], h0.at[2, own_x, behind], i=10, device=(gx, gy + 1)),
-        at1(flag_in.at[:, ny - 1], flag.at[own_x, behind], i=11, device=(gx, gy + 1)),
-    ]
+    round1[3][2] += [at1(rim_flag_out, rim_flag, i=8, device=(gx, gy + 1))]
     start(round1)
 
     loads[4].wait()
@@ -175,30 +200,42 @@
             lambda: (next_z(ex) - ex) - (e[2, ahead_x, at] - ez),
             lambda: (e[1, ahead_x, at] - ey) - (e[0, ps, nxt] - ex),
         )
-        results = []
         for c in comps:
             new = hk * src[c, ps, at] - hg * curls[c]()
-            results.append(new if keep is None else jnp.where(keep, new, 0.0))
-        for c, new in zip(comps, results):
-            dst[c, ps, at] = new
+            dst[c, ps, at] = new if keep is None else jnp.where(keep, new, 0.0)
 
     low, high = TOP, TOP + ny
     inner_end = 1 + (nx - 1) // BLOCK * BLOCK
 
     def h_inner(e, src, dst):
         def body(p, carry):
-            h_update(e, src, dst, p, BLOCK, low, ny - 8, (0, 1, 2))
+            h_update(e, src, dst, p, BLOCK, low, ny, (0, 1, 2))
             return carry
         blocks(1, inner_end, body)
 
-    def h_outer(e, src, dst):
-        def body(p, carry):
-            h_update(e, src, dst, p, BLOCK, high - 8, 8, (0, 1, 2))
-            h_update(e, src, dst, p, BLOCK, 0, 8, (0, 2), down)
-            return carry
+    def h_rows(ex, ey, ez, ey_x, ex_y, ez_y, absorbs, hx, hz):
+        hk = jnp.where(absorbs, hk1, 1.0)
+        hg = jnp.where(absorbs, hg1, DT)
+        return (hk * hx - hg * ((ez_y - ez) - (next_z(ey) - ey)),
+                hk * hz - hg * ((ey_x - ey) - (ex_y - ex)))
+
+    def h_outer(e, src, dst, down_rows, up_rows, above, below, rim):
         h_update(e, src, dst, 0, 1, low, ny, (1, 2), left)
-        h_update(e, src, dst, inner_end, nx + 1 - inner_end, low, ny - 8, (0, 1, 2))
-        blocks(1, nx + 1, body)
+        h_update(e, src, dst, inner_end, nx + 1 - inner_end, low, ny, (0, 1, 2))
+        r = high - 1
+        hx, hz = h_rows(
+            up_rows[0], up_rows[1], up_rows[2], get_rows(e, 1, 2, r), above[0], above[1],
+            get_rows(flag, 0, 1, r) == 1, get_rows(src, 0, 1, r), get_rows(src, 2, 1, r))
+        put_rows(dst, 0, 1, r, hx)
+        put_rows(dst, 2, 1, r, hz)
+        below[1, nx:nx + 1] = e[1, last, behind:behind + 1]
+        hx, hz = h_rows(
+            below[0, 0:nx], below[1, 0:nx], below[2, 0:nx], below[1, 1:nx + 1], down_rows[0], down_rows[1],
+            rim_flag[...] == 1, rim[0], rim[1])
+        hx, hz = jnp.where(down, hx, 0.0), jnp.where(down, hz, 0.0)
+        put_rows(dst, 0, 1, behind, hx)
+        put_rows(dst, 2, 1, behind, hz)
+        return hx, hz
 
     def e_update(step, src, h, dst, dst_x, dst_y, comps, p, acc):
         for r in range(0, ny, 8):
@@ -222,7 +259,6 @@
             acc = acc[:r // 8] + (piece,) + acc[r // 8 + 1:]
         return acc
 
-    loads[2].wait()
     loads[3].wait()
 
     def e_coefficients(p, carry):
@@ -240,23 +276,24 @@
         return carry
 
     blocks(0, nx, e_coefficients)
-    loads[0].wait()
-    loads[1].wait()
     h_inner(e0, h0, h1)
     wait_recv(round1)
-    h_outer(e0, h0, h1)
+    rim = h_outer(e0, h0, h1, down0, up0, above0, below0, (below0[3, 0:nx], below0[4, 0:nx]))
+    rim_h[0], rim_h[1] = rim
     acc = tuple(jnp.zeros((8, nz), jnp.float32) for _ in range(ny // 8))
     step1 = functools.partial(e_update, 0, e0, h1, e1, 0, TOP, (0, 1, 2))
-    round2 = e_halo(e1, lambda x: x + 1, lambda y: y + TOP, e1, send2, recv2)
+    round2 = e_halo(e1, down1, up1, above1, below1, send2, recv2)
     acc = step1(1, acc)
     acc = step1(nx + 1 - BLOCK, acc)
     start(round2[0:2] + round2[4:6])
     acc = blocks(1 + BLOCK, nx + 1 - BLOCK, step1, acc)
+    pack_down(e1, down1)
+    pack_up(e1, up1)
     start(round2[2:4])
 
     h_inner(e1, h1, h2)
     wait_recv(round2)
-    h_outer(e1, h1, h2)
+    h_outer(e1, h1, h2, down1, up1, above1, below1, (rim_h[0], rim_h[1]))
     step2 = functools.partial(e_update, 1, e1, h2, e_out, -1, 0)
     acc = blocks(1, nx + 1, functools.partial(step2, (0, 1)), acc)
     mine = pl.ds(pl.multiple_of(gy * ny, ny), ny)
@@ -345,6 +382,17 @@
                 h_scratch,
                 h_scratch,
                 h_scratch,
+                pltpu.VMEM((2, nx, nz), f32),
+                pltpu.VMEM((2, nx, nz), f32),
+                pltpu.VMEM((5, nx, nz), f32),
+                pltpu.VMEM((3, nx, nz), f32),
+                pltpu.VMEM((2, nx, nz), f32),
+                pltpu.VMEM((2, nx, nz), f32),
+                pltpu.VMEM((5, nx + 8, nz), f32),
+                pltpu.VMEM((3, nx + 8, nz), f32),
+                pltpu.VMEM((2, nx, nz), f32),
+                pltpu.VMEM((nx, nz), jnp.int32),
+                pltpu.VMEM((nx, nz), jnp.int32),
                 pltpu.VMEM((nx + 1, ny + 8, nz), jnp.int32),
                 pltpu.VMEM((nx, ny, nz), jnp.int32),
                 pltpu.VMEM((nx, ny, nz), f32),
@@ -353,10 +401,10 @@
                 pltpu.VMEM((1, nz), f32),
                 pltpu.SMEM((NFREQ,), f32),
                 pltpu.SemaphoreType.DMA((7,)),
-                pltpu.SemaphoreType.DMA((12,)),
-                pltpu.SemaphoreType.DMA((12,)),
-                pltpu.SemaphoreType.DMA((7,)),
-                pltpu.SemaphoreType.DMA((7,)),
+                pltpu.SemaphoreType.DMA((9,)),
+                pltpu.SemaphoreType.DMA((9,)),
+                pltpu.SemaphoreType.DMA((6,)),
+                pltpu.SemaphoreType.DMA((6,)),
                 pltpu.SemaphoreType.DMA((ngy,)),
                 pltpu.SemaphoreType.DMA((ngy,)),
             ],

time: 17.1 us -> 16.5 us (0.965)
  Pallas kernels: 16.3 us -> 15.7 us
    pallas_call x1, Pallas kernels: 15.1 us -> 14.5 us  [local(): pl.pallas_call(functools.partial(kernel, ngx, ngy, nx, ny, nz), out_shape...]
where the time goes in v4:
time: 16.5 us; the launch traced here: 16.3 us
  Pallas kernels  15.7 us (95%)
  between operations  0.64 us (4%)
    pallas_call x1, Pallas kernels, local(): pl.pallas_call(functools.partial(kernel, ngx, ngy, nx, ny, nz), out_shape...  14.5 us
    pallas_call x1, Pallas kernels, local(): pl.pallas_call(functools.partial(finish, nx), out_shape=(field, field, sp...  1.2 us

profile of v4, /device:TPU:0, one launch (start us, length us, event | category | flops | bytes accessed | tf_op | source)
XLA Modules:
  0.0 16.3 jit_solution(6898370490894097285)
XLA Ops:
  0.6 14.5 %shard_map.94 = (f32[3,32,16,128]{3,2,1,0:T(8,128)S(1)}, f32[3,32,16,128]{3,2,1,0:T(8,128)S(1)}, f32[64,128]{1,0:T(8,128)S(1)}, f32[8,128]{1,0:T(8,128)S(1)}) custom-call(f32[3,32,16,128]{3,2,1,0:T(8,128)} %e_in.1, f32[3,32,16,128]{3,2,1,0:T(8,128)} %h_in.1, s32[32,16,128]{2,1,0:T(8,128)} %mat_in.1, s32[32,16,128]{2,1,0:T(8,128)} %flag_in.1, f32[4]{0:T(128)} %perm_in.1, ...), custom_call_target="tpu_custom_call" | custom-call | tf_op jit(solution)/shard_map/pallas_call | solution.py:369
  15.1 1.2 %shard_map.95 = (f32[3,32,16,128]{3,2,1,0:T(8,128)}, f32[3,32,16,128]{3,2,1,0:T(8,128)}, f32[4,2,32,64]{3,2,1,0:T(8,128)}) custom-call(f32[3,32,16,128]{3,2,1,0:T(8,128)S(1)} %get-tuple-element.7.e_in, f32[3,32,16,128]{3,2,1,0:T(8,128)S(1)} %get-tuple-element.8.h_in, f32[64,128]{1,0:T(8,128)S(1)} %get-tuple-element.9.samp, ...), custom_call_target="tpu_custom_call" | custom-call | tf_op jit(solution)/shard_map/pallas_call | solution.py:415

commit v5 on v4

--- a/solution.py
+++ b/solution.py
@@ -28,7 +28,7 @@
 def kernel(ngx, ngy, nx, ny, nz,
            e_in, h_in, mat_in, flag_in, perm_in, sigma_in, omega_in,
            e_out, h_out, samp, weights,
-           e0, e1, h0, h1, h2, down0, down1, up0, up1, above0, above1, below0, below1, rim_h, rim_flag_out, rim_flag, flag, mat, ek, eg, perm, sigma, omega,
+           e0, e1, h0, h1, h2, down0, down1, up0, up1, above0, above1, below0, below1, rim_h, rim_flag, flag, mat, ek, eg, perm, sigma, omega,
            load_sem, send1, recv1, send2, recv2, send3, recv3):
     gx, gy = lax.axis_index("gx"), lax.axis_index("gy")
     left, right = gx > 0, gx < ngx - 1
@@ -47,8 +47,6 @@
         pltpu.make_async_copy(perm_in, perm, load_sem.at[5]),
         pltpu.make_async_copy(omega_in, omega, load_sem.at[6]),
     ]
-    for copy in loads:
-        copy.start()
 
     barrier = pltpu.get_barrier_semaphore()
     partners = [
@@ -57,7 +55,10 @@
         (left & up, (gx - 1, gy + 1)),
         (right & down, (gx + 1, gy - 1)),
     ]
-    expected = ngy - 1
+    for mate in range(ngy):
+        distance = jnp.abs(gy - mate)
+        partners.append(((distance == 1) | (distance > 3), (gx, mate)))
+    expected = 0
     for there, device in partners:
         expected = expected + there.astype(jnp.int32)
 
@@ -65,8 +66,8 @@
         def _():
             pl.semaphore_signal(barrier, inc=1, device_id=device, device_id_type=MESH)
 
-    for d in range(1, ngy):
-        pl.semaphore_signal(barrier, inc=1, device_id=(gx, lax.rem(gy + d, ngy)), device_id_type=MESH)
+    for copy in loads:
+        copy.start()
 
     @pl.when(jnp.logical_not(right))
     def _():
@@ -102,14 +103,6 @@
         for c in range(3):
             up_rows[c] = get_rows(e, c, 1, TOP + ny - 1)
 
-    for i in (0, 1, 2):
-        loads[i].wait()
-    pack_down(e0, down0)
-    pack_up(e0, up0)
-    for i, c in enumerate((0, 2)):
-        up0[3 + i] = get_rows(h0, c, 1, TOP + ny - 1)
-    rim_flag_out[...] = get_rows(flag, 0, 1, TOP + ny - 1)
-
     pl.semaphore_wait(barrier, expected)
 
     def remote(src, dst, sends, recvs, i, device):
@@ -117,15 +110,14 @@
             src_ref=src, dst_ref=dst, send_sem=sends.at[i], recv_sem=recvs.at[i],
             device_id=device, device_id_type=MESH)
 
-    def e_halo(e, down_rows, up_rows, above, below, sends, recvs):
+    def e_halo(src, e, above, below, sends, recvs):
         at = functools.partial(remote, sends=sends, recvs=recvs)
-        rim_up = TOP + ny - 1
-        to_left = [at(e.at[1:3, 1, own_y], e.at[1:3, last, own_y], i=0, device=(gx - 1, gy))]
-        to_right = [at(e.at[:, nx, own_y], e.at[:, 0, own_y], i=1, device=(gx + 1, gy))]
-        to_down = [at(down_rows, above, i=2, device=(gx, gy - 1))]
-        to_up = [at(up_rows, below.at[:, 0:nx], i=3, device=(gx, gy + 1))]
-        corner_lu = [at(e.at[1, 1, rim_up], e.at[1, last, behind], i=4, device=(gx - 1, gy + 1))]
-        corner_rd = [at(e.at[0, nx, TOP], e.at[0, 0, ahead], i=5, device=(gx + 1, gy - 1))]
+        to_left = [at(src["left"], e.at[1:3, last, own_y], i=0, device=(gx - 1, gy))]
+        to_right = [at(src["right"], e.at[:, 0, own_y], i=1, device=(gx + 1, gy))]
+        to_down = [at(rows, above.at[c], i=2 + c, device=(gx, gy - 1)) for c, rows in enumerate(src["down"])]
+        to_up = [at(src["up"], below.at[0:3, 0:nx], i=4, device=(gx, gy + 1))]
+        corner_lu = [at(src["left up"], e.at[1, last, behind], i=5, device=(gx - 1, gy + 1))]
+        corner_rd = [at(src["right down"], e.at[0, 0, ahead], i=6, device=(gx + 1, gy - 1))]
         return [
             [left, right, to_left],
             [right, left, to_right],
@@ -156,14 +148,30 @@
                 for copy in copies:
                     copy.wait_send()
 
-    round1 = e_halo(e0, down0, up0, above0, below0, send1, recv1)
+    round1 = e_halo({
+        "left": e_in.at[1:3, 0],
+        "right": e_in.at[:, nx - 1],
+        "down": [e_in.at[c, :, 0] for c in (0, 2)],
+        "up": e_in.at[:, :, ny - 1],
+        "left up": e_in.at[1, 0, ny - 1],
+        "right down": e_in.at[0, nx - 1, 0],
+    }, e0, above0, below0, send1, recv1)
     at1 = functools.partial(remote, sends=send1, recvs=recv1)
     round1[1][2] += [
-        at1(h0.at[1:3, nx, own_y], h0.at[1:3, 0, own_y], i=6, device=(gx + 1, gy)),
-        at1(flag.at[nx, own_y], flag.at[0, own_y], i=7, device=(gx + 1, gy)),
+        at1(h_in.at[1:3, nx - 1], h0.at[1:3, 0, own_y], i=7, device=(gx + 1, gy)),
+        at1(flag_in.at[nx - 1], flag.at[0, own_y], i=8, device=(gx + 1, gy)),
     ]
-    round1[3][2] += [at1(rim_flag_out, rim_flag, i=8, device=(gx, gy + 1))]
+    round1[3][2] += [
+        at1(flag_in.at[:, ny - 1], rim_flag, i=9, device=(gx, gy + 1)),
+        at1(h_in.at[0, :, ny - 1], below0.at[3, 0:nx], i=10, device=(gx, gy + 1)),
+        at1(h_in.at[2, :, ny - 1], below0.at[4, 0:nx], i=11, device=(gx, gy + 1)),
+    ]
     start(round1)
+    loads[0].wait()
+    loads[1].wait()
+    loads[2].wait()
+    pack_down(e0, down0)
+    pack_up(e0, up0)
 
     loads[4].wait()
     loads[5].wait()
@@ -282,7 +290,14 @@
     rim_h[0], rim_h[1] = rim
     acc = tuple(jnp.zeros((8, nz), jnp.float32) for _ in range(ny // 8))
     step1 = functools.partial(e_update, 0, e0, h1, e1, 0, TOP, (0, 1, 2))
-    round2 = e_halo(e1, down1, up1, above1, below1, send2, recv2)
+    round2 = e_halo({
+        "left": e1.at[1:3, 1, own_y],
+        "right": e1.at[:, nx, own_y],
+        "down": [down1.at[c] for c in range(2)],
+        "up": up1,
+        "left up": e1.at[1, 1, TOP + ny - 1],
+        "right down": e1.at[0, nx, TOP],
+    }, e1, above1, below1, send2, recv2)
     acc = step1(1, acc)
     acc = step1(nx + 1 - BLOCK, acc)
     start(round2[0:2] + round2[4:6])
@@ -384,14 +399,13 @@
                 h_scratch,
                 pltpu.VMEM((2, nx, nz), f32),
                 pltpu.VMEM((2, nx, nz), f32),
-                pltpu.VMEM((5, nx, nz), f32),
+                pltpu.VMEM((3, nx, nz), f32),
                 pltpu.VMEM((3, nx, nz), f32),
                 pltpu.VMEM((2, nx, nz), f32),
                 pltpu.VMEM((2, nx, nz), f32),
                 pltpu.VMEM((5, nx + 8, nz), f32),
                 pltpu.VMEM((3, nx + 8, nz), f32),
                 pltpu.VMEM((2, nx, nz), f32),
-                pltpu.VMEM((nx, nz), jnp.int32),
                 pltpu.VMEM((nx, nz), jnp.int32),
                 pltpu.VMEM((nx + 1, ny + 8, nz), jnp.int32),
                 pltpu.VMEM((nx, ny, nz), jnp.int32),
@@ -401,10 +415,10 @@
                 pltpu.VMEM((1, nz), f32),
                 pltpu.SMEM((NFREQ,), f32),
                 pltpu.SemaphoreType.DMA((7,)),
-                pltpu.SemaphoreType.DMA((9,)),
-                pltpu.SemaphoreType.DMA((9,)),
-                pltpu.SemaphoreType.DMA((6,)),
-                pltpu.SemaphoreType.DMA((6,)),
+                pltpu.SemaphoreType.DMA((12,)),
+                pltpu.SemaphoreType.DMA((12,)),
+                pltpu.SemaphoreType.DMA((7,)),
+                pltpu.SemaphoreType.DMA((7,)),
                 pltpu.SemaphoreType.DMA((ngy,)),
                 pltpu.SemaphoreType.DMA((ngy,)),
             ],

time: 16.5 us -> 16.7 us (1.012)
  Pallas kernels: 15.7 us -> 16 us
    pallas_call x1, Pallas kernels: 14.5 us -> 14.8 us  [local(): pl.pallas_call(functools.partial(kernel, ngx, ngy, nx, ny, nz), out_shape...]
where the time goes in v5:
time: 16.7 us; the launch traced here: 16.6 us
  Pallas kernels  16 us (96%)
  between operations  0.64 us (4%)
    pallas_call x1, Pallas kernels, local(): pl.pallas_call(functools.partial(kernel, ngx, ngy, nx, ny, nz), out_shape...  14.8 us
    pallas_call x1, Pallas kernels, local(): pl.pallas_call(functools.partial(finish, nx), out_shape=(field, field, sp...  1.2 us

profile of v5, /device:TPU:0, one launch (start us, length us, event | category | flops | bytes accessed | tf_op | source)
XLA Modules:
  0.0 16.6 jit_solution(4487286653067442990)
XLA Ops:
  0.6 14.8 %shard_map.94 = (f32[3,32,16,128]{3,2,1,0:T(8,128)S(1)}, f32[3,32,16,128]{3,2,1,0:T(8,128)S(1)}, f32[64,128]{1,0:T(8,128)S(1)}, f32[8,128]{1,0:T(8,128)S(1)}) custom-call(f32[3,32,16,128]{3,2,1,0:T(8,128)} %e_in.1, f32[3,32,16,128]{3,2,1,0:T(8,128)} %h_in.1, s32[32,16,128]{2,1,0:T(8,128)} %mat_in.1, s32[32,16,128]{2,1,0:T(8,128)} %flag_in.1, f32[4]{0:T(128)} %perm_in.1, ...), custom_call_target="tpu_custom_call" | custom-call | tf_op jit(solution)/shard_map/pallas_call | solution.py:384
  15.4 1.2 %shard_map.95 = (f32[3,32,16,128]{3,2,1,0:T(8,128)}, f32[3,32,16,128]{3,2,1,0:T(8,128)}, f32[4,2,32,64]{3,2,1,0:T(8,128)}) custom-call(f32[3,32,16,128]{3,2,1,0:T(8,128)S(1)} %get-tuple-element.7.e_in, f32[3,32,16,128]{3,2,1,0:T(8,128)S(1)} %get-tuple-element.8.h_in, f32[64,128]{1,0:T(8,128)S(1)} %get-tuple-element.9.samp, ...), custom_call_target="tpu_custom_call" | custom-call | tf_op jit(solution)/shard_map/pallas_call | solution.py:429

commit v6 on v4

--- a/solution.py
+++ b/solution.py
@@ -28,7 +28,7 @@
 def kernel(ngx, ngy, nx, ny, nz,
            e_in, h_in, mat_in, flag_in, perm_in, sigma_in, omega_in,
            e_out, h_out, samp, weights,
-           e0, e1, h0, h1, h2, down0, down1, up0, up1, above0, above1, below0, below1, rim_h, rim_flag_out, rim_flag, flag, mat, ek, eg, perm, sigma, omega,
+           e0, e1, h0, h1, h2, down0, down1, up0, up1, above0, above1, below0, below1, rim_h, right0, left0, flag, mat, ek, eg, perm, sigma, omega,
            load_sem, send1, recv1, send2, recv2, send3, recv3):
     gx, gy = lax.axis_index("gx"), lax.axis_index("gy")
     left, right = gx > 0, gx < ngx - 1
@@ -47,8 +47,6 @@
         pltpu.make_async_copy(perm_in, perm, load_sem.at[5]),
         pltpu.make_async_copy(omega_in, omega, load_sem.at[6]),
     ]
-    for copy in loads:
-        copy.start()
 
     barrier = pltpu.get_barrier_semaphore()
     partners = [
@@ -56,8 +54,12 @@
         (right, (gx + 1, gy)),
         (left & up, (gx - 1, gy + 1)),
         (right & down, (gx + 1, gy - 1)),
+        (down, (gx, gy - 1)),
+        (up, (gx, gy + 1)),
     ]
-    expected = ngy - 1
+    if ngy > 4:
+        partners += [(jnp.abs(gy - mate) > 3, (gx, mate)) for mate in range(ngy)]
+    expected = 0
     for there, device in partners:
         expected = expected + there.astype(jnp.int32)
 
@@ -65,8 +67,8 @@
         def _():
             pl.semaphore_signal(barrier, inc=1, device_id=device, device_id_type=MESH)
 
-    for d in range(1, ngy):
-        pl.semaphore_signal(barrier, inc=1, device_id=(gx, lax.rem(gy + d, ngy)), device_id_type=MESH)
+    for copy in loads:
+        copy.start()
 
     @pl.when(jnp.logical_not(right))
     def _():
@@ -108,7 +110,10 @@
     pack_up(e0, up0)
     for i, c in enumerate((0, 2)):
         up0[3 + i] = get_rows(h0, c, 1, TOP + ny - 1)
-    rim_flag_out[...] = get_rows(flag, 0, 1, TOP + ny - 1)
+    up0[5] = get_rows(flag, 0, 1, TOP + ny - 1).astype(jnp.float32)
+    right0[0:3] = e0[:, nx, own_y]
+    right0[3:5] = h0[1:3, nx, own_y]
+    right0[5] = flag[nx, own_y].astype(jnp.float32)
 
     pl.semaphore_wait(barrier, expected)
 
@@ -117,11 +122,11 @@
             src_ref=src, dst_ref=dst, send_sem=sends.at[i], recv_sem=recvs.at[i],
             device_id=device, device_id_type=MESH)
 
-    def e_halo(e, down_rows, up_rows, above, below, sends, recvs):
+    def e_halo(e, right_planes, behind_planes, down_rows, up_rows, above, below, sends, recvs):
         at = functools.partial(remote, sends=sends, recvs=recvs)
         rim_up = TOP + ny - 1
         to_left = [at(e.at[1:3, 1, own_y], e.at[1:3, last, own_y], i=0, device=(gx - 1, gy))]
-        to_right = [at(e.at[:, nx, own_y], e.at[:, 0, own_y], i=1, device=(gx + 1, gy))]
+        to_right = [at(right_planes, behind_planes, i=1, device=(gx + 1, gy))]
         to_down = [at(down_rows, above, i=2, device=(gx, gy - 1))]
         to_up = [at(up_rows, below.at[:, 0:nx], i=3, device=(gx, gy + 1))]
         corner_lu = [at(e.at[1, 1, rim_up], e.at[1, last, behind], i=4, device=(gx - 1, gy + 1))]
@@ -156,13 +161,7 @@
                 for copy in copies:
                     copy.wait_send()
 
-    round1 = e_halo(e0, down0, up0, above0, below0, send1, recv1)
-    at1 = functools.partial(remote, sends=send1, recvs=recv1)
-    round1[1][2] += [
-        at1(h0.at[1:3, nx, own_y], h0.at[1:3, 0, own_y], i=6, device=(gx + 1, gy)),
-        at1(flag.at[nx, own_y], flag.at[0, own_y], i=7, device=(gx + 1, gy)),
-    ]
-    round1[3][2] += [at1(rim_flag_out, rim_flag, i=8, device=(gx, gy + 1))]
+    round1 = e_halo(e0, right0, left0, down0, up0, above0, below0, send1, recv1)
     start(round1)
 
     loads[4].wait()
@@ -231,7 +230,7 @@
         below[1, nx:nx + 1] = e[1, last, behind:behind + 1]
         hx, hz = h_rows(
             below[0, 0:nx], below[1, 0:nx], below[2, 0:nx], below[1, 1:nx + 1], down_rows[0], down_rows[1],
-            rim_flag[...] == 1, rim[0], rim[1])
+            below0[5, 0:nx] == 1.0, rim[0], rim[1])
         hx, hz = jnp.where(down, hx, 0.0), jnp.where(down, hz, 0.0)
         put_rows(dst, 0, 1, behind, hx)
         put_rows(dst, 2, 1, behind, hz)
@@ -278,11 +277,14 @@
     blocks(0, nx, e_coefficients)
     h_inner(e0, h0, h1)
     wait_recv(round1)
+    e0[:, 0, own_y] = left0[0:3]
+    h0[1:3, 0, own_y] = left0[3:5]
+    flag[0, own_y] = left0[5].astype(jnp.int32)
     rim = h_outer(e0, h0, h1, down0, up0, above0, below0, (below0[3, 0:nx], below0[4, 0:nx]))
     rim_h[0], rim_h[1] = rim
     acc = tuple(jnp.zeros((8, nz), jnp.float32) for _ in range(ny // 8))
     step1 = functools.partial(e_update, 0, e0, h1, e1, 0, TOP, (0, 1, 2))
-    round2 = e_halo(e1, down1, up1, above1, below1, send2, recv2)
+    round2 = e_halo(e1, e1.at[:, nx, own_y], e1.at[:, 0, own_y], down1, up1, above1, below1, send2, recv2)
     acc = step1(1, acc)
     acc = step1(nx + 1 - BLOCK, acc)
     start(round2[0:2] + round2[4:6])
@@ -384,15 +386,15 @@
                 h_scratch,
                 pltpu.VMEM((2, nx, nz), f32),
                 pltpu.VMEM((2, nx, nz), f32),
-                pltpu.VMEM((5, nx, nz), f32),
+                pltpu.VMEM((6, nx, nz), f32),
                 pltpu.VMEM((3, nx, nz), f32),
                 pltpu.VMEM((2, nx, nz), f32),
                 pltpu.VMEM((2, nx, nz), f32),
-                pltpu.VMEM((5, nx + 8, nz), f32),
+                pltpu.VMEM((6, nx + 8, nz), f32),
                 pltpu.VMEM((3, nx + 8, nz), f32),
                 pltpu.VMEM((2, nx, nz), f32),
-                pltpu.VMEM((nx, nz), jnp.int32),
-                pltpu.VMEM((nx, nz), jnp.int32),
+                pltpu.VMEM((6, ny, nz), f32),
+                pltpu.VMEM((6, ny, nz), f32),
                 pltpu.VMEM((nx + 1, ny + 8, nz), jnp.int32),
                 pltpu.VMEM((nx, ny, nz), jnp.int32),
                 pltpu.VMEM((nx, ny, nz), f32),
@@ -401,8 +403,8 @@
                 pltpu.VMEM((1, nz), f32),
                 pltpu.SMEM((NFREQ,), f32),
                 pltpu.SemaphoreType.DMA((7,)),
-                pltpu.SemaphoreType.DMA((9,)),
-                pltpu.SemaphoreType.DMA((9,)),
+                pltpu.SemaphoreType.DMA((6,)),
+                pltpu.SemaphoreType.DMA((6,)),
                 pltpu.SemaphoreType.DMA((6,)),
                 pltpu.SemaphoreType.DMA((6,)),
                 pltpu.SemaphoreType.DMA((ngy,)),

time: 16.5 us -> 16.4 us (level)
  no operation moved by 1% of the time
where the time goes in v6:
time: 16.4 us; the launch traced here: 16.2 us
  Pallas kernels  15.6 us (95%)
  between operations  0.64 us (4%)
    pallas_call x1, Pallas kernels, local(): pl.pallas_call(functools.partial(kernel, ngx, ngy, nx, ny, nz), out_shape...  14.4 us
    pallas_call x1, Pallas kernels, local(): pl.pallas_call(functools.partial(finish, nx), out_shape=(field, field, sp...  1.2 us

profile of v6, /device:TPU:0, one launch (start us, length us, event | category | flops | bytes accessed | tf_op | source)
XLA Modules:
  0.0 16.2 jit_solution(15872098309163467631)
XLA Ops:
  0.6 14.4 %shard_map.94 = (f32[3,32,16,128]{3,2,1,0:T(8,128)S(1)}, f32[3,32,16,128]{3,2,1,0:T(8,128)S(1)}, f32[64,128]{1,0:T(8,128)S(1)}, f32[8,128]{1,0:T(8,128)S(1)}) custom-call(f32[3,32,16,128]{3,2,1,0:T(8,128)} %e_in.1, f32[3,32,16,128]{3,2,1,0:T(8,128)} %h_in.1, s32[32,16,128]{2,1,0:T(8,128)} %mat_in.1, s32[32,16,128]{2,1,0:T(8,128)} %flag_in.1, f32[4]{0:T(128)} %perm_in.1, ...), custom_call_target="tpu_custom_call" | custom-call | tf_op jit(solution)/shard_map/pallas_call | solution.py:371
  15.0 1.2 %shard_map.95 = (f32[3,32,16,128]{3,2,1,0:T(8,128)}, f32[3,32,16,128]{3,2,1,0:T(8,128)}, f32[4,2,32,64]{3,2,1,0:T(8,128)}) custom-call(f32[3,32,16,128]{3,2,1,0:T(8,128)S(1)} %get-tuple-element.7.e_in, f32[3,32,16,128]{3,2,1,0:T(8,128)S(1)} %get-tuple-element.8.h_in, f32[64,128]{1,0:T(8,128)S(1)} %get-tuple-element.9.samp, ...), custom_call_target="tpu_custom_call" | custom-call | tf_op jit(solution)/shard_map/pallas_call | solution.py:417

commit v7 on v6

--- a/solution.py
+++ b/solution.py
@@ -124,13 +124,12 @@
 
     def e_halo(e, right_planes, behind_planes, down_rows, up_rows, above, below, sends, recvs):
         at = functools.partial(remote, sends=sends, recvs=recvs)
-        rim_up = TOP + ny - 1
         to_left = [at(e.at[1:3, 1, own_y], e.at[1:3, last, own_y], i=0, device=(gx - 1, gy))]
         to_right = [at(right_planes, behind_planes, i=1, device=(gx + 1, gy))]
         to_down = [at(down_rows, above, i=2, device=(gx, gy - 1))]
         to_up = [at(up_rows, below.at[:, 0:nx], i=3, device=(gx, gy + 1))]
-        corner_lu = [at(e.at[1, 1, rim_up], e.at[1, last, behind], i=4, device=(gx - 1, gy + 1))]
-        corner_rd = [at(e.at[0, nx, TOP], e.at[0, 0, ahead], i=5, device=(gx + 1, gy - 1))]
+        corner_lu = [at(up_rows.at[1, 0], e.at[1, last, behind], i=4, device=(gx - 1, gy + 1))]
+        corner_rd = [at(down_rows.at[0, nx - 1], e.at[0, 0, ahead], i=5, device=(gx + 1, gy - 1))]
         return [
             [left, right, to_left],
             [right, left, to_right],
@@ -162,7 +161,7 @@
                     copy.wait_send()
 
     round1 = e_halo(e0, right0, left0, down0, up0, above0, below0, send1, recv1)
-    start(round1)
+    start(round1[4:6] + round1[0:4])
 
     loads[4].wait()
     loads[5].wait()
@@ -285,13 +284,26 @@
     acc = tuple(jnp.zeros((8, nz), jnp.float32) for _ in range(ny // 8))
     step1 = functools.partial(e_update, 0, e0, h1, e1, 0, TOP, (0, 1, 2))
     round2 = e_halo(e1, e1.at[:, nx, own_y], e1.at[:, 0, own_y], down1, up1, above1, below1, send2, recv2)
+
+    def e_rows(y, comps, out):
+        r = TOP + y
+        hx, hy, hz = (get_rows(h1, c, 1, r) for c in range(3))
+        keep, gain = get_rows(ek, 0, 0, y), get_rows(eg, 0, 0, y)
+        curls = (
+            lambda: (hz - get_rows(h1, 2, 1, r - 1)) - (hy - prev_z(hy)),
+            lambda: (hx - prev_z(hx)) - (hz - get_rows(h1, 2, 0, r)),
+            lambda: (hy - get_rows(h1, 1, 0, r)) - (hx - get_rows(h1, 0, 1, r - 1)),
+        )
+        for i, c in enumerate(comps):
+            out[i] = keep * get_rows(e0, c, 1, r) + gain * curls[c]()
+
+    e_rows(ny - 1, (0, 1, 2), up1)
+    e_rows(0, (0, 2), down1)
+    start(round2[4:6] + round2[2:4])
     acc = step1(1, acc)
     acc = step1(nx + 1 - BLOCK, acc)
-    start(round2[0:2] + round2[4:6])
+    start(round2[0:2])
     acc = blocks(1 + BLOCK, nx + 1 - BLOCK, step1, acc)
-    pack_down(e1, down1)
-    pack_up(e1, up1)
-    start(round2[2:4])
 
     h_inner(e1, h1, h2)
     wait_recv(round2)

time: 16.4 us -> 16.4 us (level)
  no operation moved by 1% of the time
where the time goes in v7:
time: 16.4 us; the launch traced here: 16.2 us
  Pallas kernels  15.6 us (95%)
  between operations  0.64 us (4%)
    pallas_call x1, Pallas kernels, local(): pl.pallas_call(functools.partial(kernel, ngx, ngy, nx, ny, nz), out_shape...  14.4 us
    pallas_call x1, Pallas kernels, local(): pl.pallas_call(functools.partial(finish, nx), out_shape=(field, field, sp...  1.2 us

profile of v7, /device:TPU:0, one launch (start us, length us, event | category | flops | bytes accessed | tf_op | source)
XLA Modules:
  0.0 16.2 jit_solution(14451996495413224574)
XLA Ops:
  0.6 14.4 %shard_map.94 = (f32[3,32,16,128]{3,2,1,0:T(8,128)S(1)}, f32[3,32,16,128]{3,2,1,0:T(8,128)S(1)}, f32[64,128]{1,0:T(8,128)S(1)}, f32[8,128]{1,0:T(8,128)S(1)}) custom-call(f32[3,32,16,128]{3,2,1,0:T(8,128)} %e_in.1, f32[3,32,16,128]{3,2,1,0:T(8,128)} %h_in.1, s32[32,16,128]{2,1,0:T(8,128)} %mat_in.1, s32[32,16,128]{2,1,0:T(8,128)} %flag_in.1, f32[4]{0:T(128)} %perm_in.1, ...), custom_call_target="tpu_custom_call" | custom-call | tf_op jit(solution)/shard_map/pallas_call | solution.py:383
  15.0 1.2 %shard_map.95 = (f32[3,32,16,128]{3,2,1,0:T(8,128)}, f32[3,32,16,128]{3,2,1,0:T(8,128)}, f32[4,2,32,64]{3,2,1,0:T(8,128)}) custom-call(f32[3,32,16,128]{3,2,1,0:T(8,128)S(1)} %get-tuple-element.7.e_in, f32[3,32,16,128]{3,2,1,0:T(8,128)S(1)} %get-tuple-element.8.h_in, f32[64,128]{1,0:T(8,128)S(1)} %get-tuple-element.9.samp, ...), custom_call_target="tpu_custom_call" | custom-call | tf_op jit(solution)/shard_map/pallas_call | solution.py:429

commit v8 on v7

--- a/solution.py
+++ b/solution.py
@@ -20,7 +20,14 @@
 
 
 def blocks(low, high, body, carry=0):
-    for p in range(low, high, BLOCK):
+    pairs = (high - low) // (2 * BLOCK)
+
+    def pair(i, carry):
+        p = low + i * (2 * BLOCK)
+        return body(p + BLOCK, body(p, carry))
+
+    carry = lax.fori_loop(0, pairs, pair, carry)
+    for p in range(low + pairs * 2 * BLOCK, high, BLOCK):
         carry = body(p, carry)
     return carry
 

time: 16.4 us -> 16.3 us (level)
  no operation moved by 1% of the time
where the time goes in v8:
time: 16.3 us; the launch traced here: 16.1 us
  Pallas kernels  15.5 us (95%)
  between operations  0.64 us (4%)
    pallas_call x1, Pallas kernels, local(): pl.pallas_call(functools.partial(kernel, ngx, ngy, nx, ny, nz), out_shape...  14.3 us
    pallas_call x1, Pallas kernels, local(): pl.pallas_call(functools.partial(finish, nx), out_shape=(field, field, sp...  1.2 us

profile of v8, /device:TPU:0, one launch (start us, length us, event | category | flops | bytes accessed | tf_op | source)
XLA Modules:
  0.0 16.1 jit_solution(14733559535531841894)
XLA Ops:
  0.6 14.3 %shard_map.94 = (f32[3,32,16,128]{3,2,1,0:T(8,128)S(1)}, f32[3,32,16,128]{3,2,1,0:T(8,128)S(1)}, f32[64,128]{1,0:T(8,128)S(1)}, f32[8,128]{1,0:T(8,128)S(1)}) custom-call(f32[3,32,16,128]{3,2,1,0:T(8,128)} %e_in.1, f32[3,32,16,128]{3,2,1,0:T(8,128)} %h_in.1, s32[32,16,128]{2,1,0:T(8,128)} %mat_in.1, s32[32,16,128]{2,1,0:T(8,128)} %flag_in.1, f32[4]{0:T(128)} %perm_in.1, ...), custom_call_target="tpu_custom_call" | custom-call | tf_op jit(solution)/shard_map/pallas_call | solution.py:390
  14.9 1.2 %shard_map.95 = (f32[3,32,16,128]{3,2,1,0:T(8,128)}, f32[3,32,16,128]{3,2,1,0:T(8,128)}, f32[4,2,32,64]{3,2,1,0:T(8,128)}) custom-call(f32[3,32,16,128]{3,2,1,0:T(8,128)S(1)} %get-tuple-element.7.e_in, f32[3,32,16,128]{3,2,1,0:T(8,128)S(1)} %get-tuple-element.8.h_in, f32[64,128]{1,0:T(8,128)S(1)} %get-tuple-element.9.samp, ...), custom_call_target="tpu_custom_call" | custom-call | tf_op jit(solution)/shard_map/pallas_call | solution.py:436

commit v9 on v7

--- a/solution.py
+++ b/solution.py
@@ -20,8 +20,11 @@
 
 
 def blocks(low, high, body, carry=0):
-    for p in range(low, high, BLOCK):
-        carry = body(p, carry)
+    rounds = (high - low) // BLOCK
+    carry = lax.fori_loop(0, rounds, lambda i, c: body(low + i * BLOCK, c), carry)
+    rest = low + rounds * BLOCK
+    if rest < high:
+        carry = body(rest, carry, high - rest)
     return carry
 
 
@@ -81,10 +84,6 @@
         for e, above in ((e0, above0), (e1, above1)):
             e[0, 0, ahead:ahead + 8] = jnp.zeros((8, nz), jnp.float32)
             above[...] = jnp.zeros((2, nx, nz), jnp.float32)
-
-    for e in (e0, e1):
-        for c in (0, 2):
-            e[c, 1:last, ahead:ahead + 8] = jnp.zeros((nx, 8, nz), jnp.float32)
 
     def row_of(ref, c, first, r):
         planes, rows = ref.shape[-3], ref.shape[-2]
@@ -206,8 +205,8 @@
     inner_end = 1 + (nx - 1) // BLOCK * BLOCK
 
     def h_inner(e, src, dst):
-        def body(p, carry):
-            h_update(e, src, dst, p, BLOCK, low, ny, (0, 1, 2))
+        def body(p, carry, planes=BLOCK):
+            h_update(e, src, dst, p, planes, low, ny, (0, 1, 2))
             return carry
         blocks(1, inner_end, body)
 
@@ -235,10 +234,10 @@
         put_rows(dst, 2, 1, behind, hz)
         return hx, hz
 
-    def e_update(step, src, h, dst, dst_x, dst_y, comps, p, acc):
+    def e_update(step, src, h, dst, dst_x, dst_y, comps, p, acc, planes=BLOCK):
         for r in range(0, ny, 8):
             at, below = slice(low + r, low + r + 8), slice(low + r - 1, low + r + 7)
-            ps, behind_x = pl.ds(p, BLOCK), pl.ds(p - 1, BLOCK)
+            ps, behind_x = pl.ds(p, planes), pl.ds(p - 1, planes)
             hx, hy, hz = h[0, ps, at], h[1, ps, at], h[2, ps, at]
             keep, gain = ek[behind_x, r:r + 8], eg[behind_x, r:r + 8]
             curls = (
@@ -248,10 +247,10 @@
             )
             news = {c: keep * src[c, ps, at] + gain * curls[c]() for c in comps}
             for c in comps:
-                dst[c, pl.ds(p + dst_x, BLOCK), r + dst_y:r + dst_y + 8] = news[c]
+                dst[c, pl.ds(p + dst_x, planes), r + dst_y:r + dst_y + 8] = news[c]
             piece = acc[r // 8]
             for c in (c for c in comps if c < 2):
-                for k in range(BLOCK):
+                for k in range(planes):
                     column = jnp.broadcast_to(news[c][k, :, nz // 2:nz // 2 + 1], (8, nz))
                     piece = jnp.where(lanes(piece) == (step * 2 + c) * nx + p - 1 + k, column, piece)
             acc = acc[:r // 8] + (piece,) + acc[r // 8 + 1:]
@@ -297,17 +296,19 @@
         for i, c in enumerate(comps):
             out[i] = keep * get_rows(e0, c, 1, r) + gain * curls[c]()
 
+    acc = step1(1, acc, 1)
+    acc = step1(nx, acc, 1)
+    start(round2[0:2])
     e_rows(ny - 1, (0, 1, 2), up1)
     e_rows(0, (0, 2), down1)
     start(round2[4:6] + round2[2:4])
-    acc = step1(1, acc)
-    acc = step1(nx + 1 - BLOCK, acc)
-    start(round2[0:2])
-    acc = blocks(1 + BLOCK, nx + 1 - BLOCK, step1, acc)
+    acc = blocks(2, nx, step1, acc)
 
     h_inner(e1, h1, h2)
     wait_recv(round2)
     h_outer(e1, h1, h2, down1, up1, above1, below1, (rim_h[0], rim_h[1]))
+    h_copy = pltpu.make_async_copy(h2.at[:, own_x, own_y], h_out, load_sem.at[7])
+    h_copy.start()
     step2 = functools.partial(e_update, 1, e1, h2, e_out, -1, 0)
     acc = blocks(1, nx + 1, functools.partial(step2, (0, 1)), acc)
     mine = pl.ds(pl.multiple_of(gy * ny, ny), ny)
@@ -321,7 +322,6 @@
         copy.start()
         round3.append(copy)
     blocks(1, nx + 1, functools.partial(step2, (2,)), acc)
-    h_out[...] = h2[:, 1:nx + 1, low:high]
     loads[6].wait()
     slots = 2 * NFREQ // ngy
     rows = lax.broadcasted_iota(jnp.int32, (8, nz), 0)
@@ -340,6 +340,7 @@
         copy.wait_recv()
     for copy in round3:
         copy.wait_send()
+    h_copy.wait()
 
 
 def finish(nx, e_in, h_in, samp, weights, e_out, h_out, spectra_out, spectra, sems):
@@ -414,7 +415,7 @@
                 pltpu.SMEM((NMAT,), f32),
                 pltpu.VMEM((1, nz), f32),
                 pltpu.SMEM((NFREQ,), f32),
-                pltpu.SemaphoreType.DMA((7,)),
+                pltpu.SemaphoreType.DMA((8,)),
                 pltpu.SemaphoreType.DMA((6,)),
                 pltpu.SemaphoreType.DMA((6,)),
                 pltpu.SemaphoreType.DMA((6,)),

time: 16.4 us -> 16.7 us (1.018)
  Pallas kernels: 15.6 us -> 15.9 us
    pallas_call x1, Pallas kernels: 14.4 us -> 14.7 us  [local(): pl.pallas_call(functools.partial(kernel, ngx, ngy, nx, ny, nz), out_shape...]
where the time goes in v9:
time: 16.7 us; the launch traced here: 16.6 us
  Pallas kernels  15.9 us (95%)
  between operations  0.64 us (4%)
    pallas_call x1, Pallas kernels, local(): pl.pallas_call(functools.partial(kernel, ngx, ngy, nx, ny, nz), out_shape...  14.7 us
    pallas_call x1, Pallas kernels, local(): pl.pallas_call(functools.partial(finish, nx), out_shape=(field, field, sp...  1.2 us

profile of v9, /device:TPU:0, one launch (start us, length us, event | category | flops | bytes accessed | tf_op | source)
XLA Modules:
  0.0 16.6 jit_solution(17555561714555518955)
XLA Ops:
  0.6 14.7 %shard_map.94 = (f32[3,32,16,128]{3,2,1,0:T(8,128)S(1)}, f32[3,32,16,128]{3,2,1,0:T(8,128)S(1)}, f32[64,128]{1,0:T(8,128)S(1)}, f32[8,128]{1,0:T(8,128)S(1)}) custom-call(f32[3,32,16,128]{3,2,1,0:T(8,128)} %e_in.1, f32[3,32,16,128]{3,2,1,0:T(8,128)} %h_in.1, s32[32,16,128]{2,1,0:T(8,128)} %mat_in.1, s32[32,16,128]{2,1,0:T(8,128)} %flag_in.1, f32[4]{0:T(128)} %perm_in.1, ...), custom_call_target="tpu_custom_call" | custom-call | tf_op jit(solution)/shard_map/pallas_call | solution.py:384
  15.4 1.2 %shard_map.95 = (f32[3,32,16,128]{3,2,1,0:T(8,128)}, f32[3,32,16,128]{3,2,1,0:T(8,128)}, f32[4,2,32,64]{3,2,1,0:T(8,128)}) custom-call(f32[3,32,16,128]{3,2,1,0:T(8,128)S(1)} %get-tuple-element.7.e_in, f32[3,32,16,128]{3,2,1,0:T(8,128)S(1)} %get-tuple-element.8.h_in, f32[64,128]{1,0:T(8,128)S(1)} %get-tuple-element.9.samp, ...), custom_call_target="tpu_custom_call" | custom-call | tf_op jit(solution)/shard_map/pallas_call | solution.py:430

commit v10 on v8

--- a/solution.py
+++ b/solution.py
@@ -304,12 +304,12 @@
         for i, c in enumerate(comps):
             out[i] = keep * get_rows(e0, c, 1, r) + gain * curls[c]()
 
+    acc = step1(1, acc)
+    acc = step1(nx + 1 - BLOCK, acc)
+    start(round2[0:2])
     e_rows(ny - 1, (0, 1, 2), up1)
     e_rows(0, (0, 2), down1)
     start(round2[4:6] + round2[2:4])
-    acc = step1(1, acc)
-    acc = step1(nx + 1 - BLOCK, acc)
-    start(round2[0:2])
     acc = blocks(1 + BLOCK, nx + 1 - BLOCK, step1, acc)
 
     h_inner(e1, h1, h2)

time: 16.3 us -> 16.1 us (0.988)
  no operation moved by 1% of the time
where the time goes in v10:
time: 16.1 us; the launch traced here: 16 us
  Pallas kernels  15.4 us (96%)
  between operations  0.64 us (4%)
    pallas_call x1, Pallas kernels, local(): pl.pallas_call(functools.partial(kernel, ngx, ngy, nx, ny, nz), out_shape...  14.2 us
    pallas_call x1, Pallas kernels, local(): pl.pallas_call(functools.partial(finish, nx), out_shape=(field, field, sp...  1.2 us

profile of v10, /device:TPU:0, one launch (start us, length us, event | category | flops | bytes accessed | tf_op | source)
XLA Modules:
  0.0 16.0 jit_solution(4416524421715984049)
XLA Ops:
  0.6 14.2 %shard_map.94 = (f32[3,32,16,128]{3,2,1,0:T(8,128)S(1)}, f32[3,32,16,128]{3,2,1,0:T(8,128)S(1)}, f32[64,128]{1,0:T(8,128)S(1)}, f32[8,128]{1,0:T(8,128)S(1)}) custom-call(f32[3,32,16,128]{3,2,1,0:T(8,128)} %e_in.1, f32[3,32,16,128]{3,2,1,0:T(8,128)} %h_in.1, s32[32,16,128]{2,1,0:T(8,128)} %mat_in.1, s32[32,16,128]{2,1,0:T(8,128)} %flag_in.1, f32[4]{0:T(128)} %perm_in.1, ...), custom_call_target="tpu_custom_call" | custom-call | tf_op jit(solution)/shard_map/pallas_call | solution.py:390
  14.8 1.2 %shard_map.95 = (f32[3,32,16,128]{3,2,1,0:T(8,128)}, f32[3,32,16,128]{3,2,1,0:T(8,128)}, f32[4,2,32,64]{3,2,1,0:T(8,128)}) custom-call(f32[3,32,16,128]{3,2,1,0:T(8,128)S(1)} %get-tuple-element.7.e_in, f32[3,32,16,128]{3,2,1,0:T(8,128)S(1)} %get-tuple-element.8.h_in, f32[64,128]{1,0:T(8,128)S(1)} %get-tuple-element.9.samp, ...), custom_call_target="tpu_custom_call" | custom-call | tf_op jit(solution)/shard_map/pallas_call | solution.py:436
